TPU v7x, 32 devices: a whole 2x2x4 slice. The times are simulated.
32 devices in a mesh: ep: 8 (over y, x, core), hs: 4 (over z).
Axes of the slice: x: 2, y: 2, z: 4, core: 2. Of those that a mesh axis runs over, the one named last changes fastest.
Arguments:
- tokens: bfloat16 [8192, 1152], P(('ep', 'hs')), may hold values from -6 to 6
- starts: int32 [8192], P(('ep', 'hs')), may hold values from 0 to 1, as said below
- counts: int32 [32], P(('ep', 'hs')), may hold values from 192 to 256, as said below
- routes: int32 [8192], P(('ep', 'hs')), may hold values from 0 to 7
- slot_index: int32 [8192], P(('ep', 'hs')), may hold values from -1 to 39, as said below
- gain_mix: float32 [1152], replicated, may hold values from 0.5 to 1.5
- in_proj: bfloat16 [1152, 4608], replicated, may hold values from -0.1875 to 0.1875
- conv_weight: float32 [4, 2304], replicated, may hold values from -3 to 3
- conv_bias: float32 [2304], replicated, may hold values from -3 to 3
- x_proj: bfloat16 [2304, 104], replicated, may hold values from -1 to 1
- dt_proj: bfloat16 [72, 2304], replicated, may hold values from -0.75 to 0.75
- dt_bias: float32 [2304], replicated, may hold values from -12 to 0
- a_log: float32 [2304, 16], replicated, may hold values from -3 to -1
- skip_gain: float32 [2304], replicated, may hold values from 0.5 to 1.5
- out_proj: bfloat16 [2304, 1152], replicated, may hold values from -0.375 to 0.375
- gain_ffn: float32 [1152], replicated, may hold values from 0.5 to 1.5
- router: float32 [1152, 8], replicated, may hold values from -0.125 to 0.125
- up_proj: bfloat16 [8, 1152, 3072], P('ep', None, 'hs'), may hold values from -0.1875 to 0.1875
- down_proj: bfloat16 [8, 3072, 1152], P('ep', 'hs'), may hold values from -0.875 to 0.875
- out_grad: bfloat16 [8192, 1152], P(('ep', 'hs')), may hold values from -6 to 6
Outputs:
- block_out: bfloat16 [8192, 1152], P(('ep', 'hs'))
- tokens_grad: float32 [8192, 1152], P(('ep', 'hs'))
- gains_grad: float32 [2304], P(('ep', 'hs'))
- router_grad: float32 [9216], P(('ep', 'hs'))
- in_proj_grad: float32 [1152, 4608], P(None, ('ep', 'hs'))
- conv_weight_grad: float32 [4, 2304], P(None, ('ep', 'hs'))
- conv_bias_grad: float32 [2304], P(('ep', 'hs'))
- x_proj_grad: float32 [2304, 104], P(('ep', 'hs'))
- dt_proj_grad: float32 [72, 2304], P(None, ('ep', 'hs'))
- dt_bias_grad: float32 [2304], P(('ep', 'hs'))
- a_log_grad: float32 [2304, 16], P(('ep', 'hs'))
- skip_gain_grad: float32 [2304], P(('ep', 'hs'))
- out_proj_grad: float32 [2304, 1152], P(('ep', 'hs'))
- up_proj_grad: float32 [8, 1152, 3072], P('ep', None, 'hs')
- down_proj_grad: float32 [8, 3072, 1152], P('ep', 'hs')
Inputs may be any that keep to these rules, and one draw needn't show every extreme that they name: `starts`: 1 exactly at the first real row of each sequence, 0 elsewhere; the real rows of the 4 devices of one index of ep, in device order, form three whole sequences, the first starting at the group's first real row and the second having real rows on every one of these devices. `counts`: a device's real rows are its first rows, the rest is padding. `slot_index`: -1 on padding rows and where a device has already given 40 earlier real rows to the same expert; else the number of earlier real rows of the same device with the same route.
All inputs are finite; a program needn't handle non-finite values.
Results may differ from a plain program's by a relative error of at most 0.012.
The roundings to bfloat16 on the way count: a program that leaves them out, or rounds other values in their place, can miss the bound.
Values may be sent and summed in bfloat16 or wider, within the bound.
No kernel may reach another device: no remote copies, remote signals or barrier semaphores. Data moves between devices by JAX's collectives and lax.ppermute only.
A program may use at most 448 MiB of HBM per device.

v0:
```python
import jax
import jax.numpy as jnp
from jax import lax
from jax.sharding import PartitionSpec as P

DT_RANK = 72
STATE = 16
CONV = 4
SCAN_BLOCK = 16


norm_epsilon = 1e-05
highest = lax.Precision.HIGHEST


def shifted_2(block, axis, distance):
    devices = range(lax.axis_size(axis))
    route = [(i - distance, i) for i in devices if i - distance in devices]
    return lax.ppermute(block, axis, route)


def entering(value, axis, join, neutral):
    count, mine = (lax.axis_size(axis), lax.axis_index(axis))
    pieces = jax.tree.map(lambda part: lax.all_gather(part, axis), value)
    so_far = jax.tree.map(
        lambda part, zero: jnp.full_like(part, 0) + jnp.asarray(zero, part.dtype), value, neutral
    )

    def step(position, so_far):
        longer = join(so_far, jax.tree.map(lambda part: part[position], pieces))
        return jax.tree.map(lambda new, old: jnp.where(position < mine, new, old), longer, so_far)

    return lax.fori_loop(0, count - 1, step, so_far)


def entering_2(array, axis, join, neutral):
    count = lax.axis_size(axis)
    place = lax.axis_index(axis)
    ahead = count - 1 - place
    gathered = jax.tree.map(
        lambda a, kind: lax.all_gather(a.astype(kind), axis),
        array,
        jax.tree.map(lambda a: jnp.bfloat16 if a.dtype == jnp.float32 else a.dtype, array),
    )
    state = jax.tree.map(lambda a, e: jnp.zeros_like(a) + jnp.asarray(e, a.dtype), array, neutral)

    def one(step, state):
        source = count - 1 - step
        return join(
            state,
            jax.tree.map(
                lambda a, own: lax.dynamic_index_in_dim(a, source, 0, False).astype(own.dtype),
                gathered,
                array,
            ),
        )

    return lax.fori_loop(0, ahead, one, state)


def rms_scale(values):
    return lax.rsqrt(jnp.mean(values * values, axis=1, keepdims=True) + norm_epsilon)


def scaled_norm(values, gain_row):
    return values * rms_scale(values) * gain_row[None, :]


def gelu_tanh(values):
    return jax.nn.gelu(values, approximate=True)


def join_forward(earlier, latter):
    return (earlier[0] * latter[0], latter[0] * earlier[1] + latter[1])


def join_backward(earlier, latter):
    return (latter[0] * earlier[0], latter[1] + latter[0] * earlier[1])


def conv_mix(x_inner, halo_rows, halo_flags, start_flags, conv_w, conv_b):
    tap_count = conv_w.shape[0]
    length = x_inner.shape[0]
    extended = jnp.concatenate([halo_rows, x_inner], axis=0)
    flag_line = jnp.concatenate([halo_flags, start_flags], axis=0)
    result = conv_b[None, :] + conv_w[tap_count - 1][None, :] * x_inner
    survive = jnp.ones((length,), jnp.float32)
    for offset in range(1, tap_count):
        survive = survive * (1.0 - flag_line[tap_count - offset : tap_count - offset + length])
        shifted = extended[tap_count - 1 - offset : tap_count - 1 - offset + length]
        result = result + conv_w[tap_count - 1 - offset][None, :] * shifted * survive[:, None]
    return jax.nn.silu(result)


def delta_apply(step_pre, bias_row, real_rows):
    return jax.nn.softplus(step_pre + bias_row[None, :]) * real_rows[:, None]


def block_view(values, block_size):
    blocked = values.reshape((values.shape[0] // block_size, block_size) + values.shape[1:])
    return jnp.swapaxes(blocked, 0, 1)


def block_summaries(mixer_in, step_size, input_map, start_flags, log_rates, block_size):
    rate_table = -jnp.exp(log_rates)
    blocks = mixer_in.shape[0] // block_size
    staying = 1.0 - start_flags
    sequence = (
        block_view(mixer_in * step_size, block_size),
        block_view(step_size, block_size),
        block_view(input_map, block_size),
        block_view(staying, block_size),
    )

    def advance(memory, element):
        driven, stride, in_map, remain = element
        decays = jnp.exp(stride[:, :, None] * rate_table[None]) * remain[:, None, None]
        return (decays * memory + driven[:, :, None] * in_map[:, None, :], None)

    initial = jnp.zeros((blocks,) + rate_table.shape, jnp.float32)
    block_ends, _ = lax.scan(jax.checkpoint(advance), initial, sequence)
    stride_total = jnp.sum(step_size.reshape(blocks, block_size, -1), axis=1)
    kept_total = jnp.prod(staying.reshape(blocks, block_size), axis=1)
    block_spans = jnp.exp(stride_total[:, :, None] * rate_table[None]) * kept_total[:, None, None]
    return lax.associative_scan(join_forward, (block_spans, block_ends), axis=0)


def block_outputs(
    mixer_in,
    step_size,
    input_map,
    output_map,
    start_flags,
    log_rates,
    skip_w,
    gate_pre,
    spans_cum,
    ends_cum,
    state_in,
    block_size,
):
    rate_table = -jnp.exp(log_rates)
    staying = 1.0 - start_flags
    first_span = jnp.ones((1,) + rate_table.shape, jnp.float32)
    first_end = jnp.zeros((1,) + rate_table.shape, jnp.float32)
    prior_span = jnp.concatenate([first_span, spans_cum[:-1]], axis=0)
    prior_end = jnp.concatenate([first_end, ends_cum[:-1]], axis=0)
    opening = prior_span * state_in[None] + prior_end
    sequence = (
        block_view(mixer_in * step_size, block_size),
        block_view(step_size, block_size),
        block_view(input_map, block_size),
        block_view(output_map, block_size),
        block_view(staying, block_size),
    )

    def advance(memory, element):
        driven, stride, in_map, out_map, remain = element
        decays = jnp.exp(stride[:, :, None] * rate_table[None]) * remain[:, None, None]
        memory = decays * memory + driven[:, :, None] * in_map[:, None, :]
        return (memory, jnp.sum(memory * out_map[:, None, :], axis=2))

    _, readout = lax.scan(jax.checkpoint(advance), opening, sequence)
    scan_out = jnp.swapaxes(readout, 0, 1).reshape(mixer_in.shape) + skip_w[None, :] * mixer_in
    return scan_out * jax.nn.silu(gate_pre)


def body(
    tokens,
    starts,
    counts,
    routes,
    slot_index,
    gain_mix,
    in_proj,
    conv_weight,
    conv_bias,
    x_proj,
    dt_proj,
    dt_bias,
    a_log,
    skip_gain,
    out_proj,
    gain_ffn,
    router,
    up_proj,
    down_proj,
    out_grad,
):
    float_type = jnp.float32
    low_type = jnp.bfloat16
    rows_first = (((0,), (0,)), ((), ()))
    last_dims = (((1,), (1,)), ((), ()))
    length = tokens.shape[0]
    model_width = tokens.shape[1]
    inner_width = conv_bias.shape[0]
    experts = router.shape[1]
    capacity = 5 * length // (4 * experts)
    edge_start = counts[0] - (CONV - 1)
    start_flags = starts.astype(float_type)
    real_rows = (jnp.arange(length, dtype=jnp.int32) < counts[0]).astype(float_type)
    tokens_float = tokens.astype(float_type)
    normed_one, norm_one_back = jax.vjp(scaled_norm, tokens_float, gain_mix)
    normed_low = normed_one.astype(low_type)
    projected = jnp.dot(normed_low, in_proj, preferred_element_type=float_type)
    inner_x = projected[:, :inner_width]
    inner_gate = projected[:, inner_width:]
    edge_rows = lax.dynamic_slice_in_dim(inner_x, edge_start, CONV - 1, 0)
    edge_flags = lax.dynamic_slice_in_dim(start_flags, edge_start, CONV - 1, 0)
    halo_rows, halo_flags = shifted_2((edge_rows, edge_flags), "hs", 1)

    def conv_part(x_part, rows_part, weight_part, bias_part):
        return conv_mix(x_part, rows_part, halo_flags, start_flags, weight_part, bias_part)

    mixer_in, conv_back = jax.vjp(conv_part, inner_x, halo_rows, conv_weight, conv_bias)
    mixer_low = mixer_in.astype(low_type)
    small_proj = jnp.dot(mixer_low, x_proj, preferred_element_type=float_type)
    rank_low = small_proj[:, :DT_RANK].astype(low_type)
    step_pre = jnp.dot(rank_low, dt_proj, preferred_element_type=float_type)
    input_map = small_proj[:, DT_RANK : DT_RANK + STATE]
    output_map = small_proj[:, DT_RANK + STATE :]

    def step_part(pre_part, bias_part):
        return delta_apply(pre_part, bias_part, real_rows)

    step_size, step_back = jax.vjp(step_part, step_pre, dt_bias)

    def summary_part(in_part, size_part, map_part, log_part):
        return block_summaries(in_part, size_part, map_part, start_flags, log_part, SCAN_BLOCK)

    (spans_cum, ends_cum), summary_back = jax.vjp(
        summary_part, mixer_in, step_size, input_map, a_log
    )
    span_device = spans_cum[-1]
    end_device = ends_cum[-1]
    unit_span = jnp.ones_like(span_device)
    zero_state = jnp.zeros_like(end_device)
    _, state_in = entering((span_device, end_device), "hs", join_forward, (unit_span, zero_state))

    def output_part(
        in_part,
        size_part,
        in_map,
        out_map,
        log_part,
        skip_part,
        gate_part,
        span_part,
        end_part,
        state_part,
    ):
        return block_outputs(
            in_part,
            size_part,
            in_map,
            out_map,
            start_flags,
            log_part,
            skip_part,
            gate_part,
            span_part,
            end_part,
            state_part,
            SCAN_BLOCK,
        )

    gated_out, output_back = jax.vjp(
        output_part,
        mixer_in,
        step_size,
        input_map,
        output_map,
        a_log,
        skip_gain,
        inner_gate,
        spans_cum,
        ends_cum,
        state_in,
    )
    gated_low = gated_out.astype(low_type)
    mixer_out = jnp.dot(gated_low, out_proj, preferred_element_type=float_type)
    middle = tokens_float + mixer_out * real_rows[:, None]
    normed_two, norm_two_back = jax.vjp(scaled_norm, middle, gain_ffn)
    router_probs = jax.nn.softmax(
        jnp.dot(normed_two, router, precision=highest, preferred_element_type=float_type), axis=1
    )
    chosen = (routes[:, None] == jnp.arange(experts, dtype=jnp.int32)[None, :]).astype(float_type)
    gate_value = jnp.sum(router_probs * chosen, axis=1)
    column = routes * capacity + slot_index
    placed = (
        (column[:, None] == jnp.arange(experts * capacity, dtype=jnp.int32)[None, :])
        & (slot_index[:, None] >= 0)
    ).astype(low_type)
    dispatched = lax.dot_general(
        placed, normed_two.astype(low_type), rows_first, preferred_element_type=float_type
    ).astype(low_type)
    arrived = lax.all_to_all(
        dispatched.reshape(experts, capacity, model_width),
        "ep",
        split_axis=0,
        concat_axis=0,
        tiled=True,
    )
    gathered_rows = lax.all_gather(arrived, "hs", axis=0, tiled=True).reshape(-1, model_width)
    hidden_pre = jnp.dot(gathered_rows, up_proj[0], preferred_element_type=float_type)
    hidden, gelu_back = jax.vjp(gelu_tanh, hidden_pre)
    hidden_low = hidden.astype(low_type)
    partial_out = jnp.dot(hidden_low, down_proj[0], preferred_element_type=float_type)
    returned = lax.psum_scatter(partial_out, "hs", scatter_dimension=0, tiled=True).astype(low_type)
    home_rows = lax.all_to_all(
        returned.reshape(-1, capacity, model_width), "ep", split_axis=0, concat_axis=0, tiled=True
    )
    expert_out = jnp.dot(
        placed,
        home_rows.reshape(experts * capacity, model_width),
        preferred_element_type=float_type,
    )
    block_out = (middle + gate_value[:, None] * expert_out).astype(low_type)
    grad_out = out_grad.astype(float_type)
    gate_grad = jnp.sum(grad_out * expert_out, axis=1)
    token_grad = grad_out * gate_value[:, None]
    placed_full = placed.astype(float_type)
    rows_grad = lax.dot_general(
        placed_full, token_grad, rows_first, precision=highest, preferred_element_type=float_type
    ).astype(low_type)
    arrived_grad = lax.all_to_all(
        rows_grad.reshape(experts, capacity, model_width),
        "ep",
        split_axis=0,
        concat_axis=0,
        tiled=True,
    )
    gathered_grad = lax.all_gather(arrived_grad, "hs", axis=0, tiled=True).reshape(-1, model_width)
    hidden_grad = lax.dot_general(
        gathered_grad, down_proj[0], last_dims, preferred_element_type=float_type
    )
    down_grad = lax.dot_general(
        hidden_low, gathered_grad, rows_first, preferred_element_type=float_type
    )
    pre_grad = gelu_back(hidden_grad)[0].astype(low_type)
    up_grad = lax.dot_general(
        gathered_rows, pre_grad, rows_first, preferred_element_type=float_type
    )
    partial_grad = lax.dot_general(
        pre_grad, up_proj[0], last_dims, preferred_element_type=float_type
    )
    own_grad = (
        lax.psum_scatter(partial_grad.astype(jnp.bfloat16), "hs", scatter_dimension=0, tiled=True)
        .astype(jnp.float32)
        .astype(low_type)
    )
    home_grad = lax.all_to_all(
        own_grad.reshape(-1, capacity, model_width), "ep", split_axis=0, concat_axis=0, tiled=True
    )
    normed_two_grad = jnp.dot(
        placed_full,
        home_grad.reshape(experts * capacity, model_width).astype(float_type),
        precision=highest,
        preferred_element_type=float_type,
    )
    logit_grad = router_probs * gate_grad[:, None] * (chosen - gate_value[:, None])
    router_grad = lax.dot_general(
        normed_two, logit_grad, rows_first, precision=highest, preferred_element_type=float_type
    )
    normed_two_grad = normed_two_grad + lax.dot_general(
        logit_grad, router, last_dims, precision=highest, preferred_element_type=float_type
    )
    middle_norm_grad, gain_ffn_grad = norm_two_back(normed_two_grad)
    middle_grad = grad_out + middle_norm_grad
    mixer_grad = (middle_grad * real_rows[:, None]).astype(low_type)
    out_proj_grad = lax.dot_general(
        gated_low, mixer_grad, rows_first, preferred_element_type=float_type
    )
    gated_grad = lax.dot_general(mixer_grad, out_proj, last_dims, preferred_element_type=float_type)
    (
        scan_in_grad,
        size_grad_two,
        in_map_grad_two,
        out_map_grad,
        log_grad_two,
        skip_grad,
        gate_pre_grad,
        span_grad,
        end_grad,
        state_grad,
    ) = output_back(gated_grad)
    _, carried_grad = entering_2(
        (span_device, state_grad), "hs", join_backward, (unit_span, zero_state)
    )
    span_grad = span_grad.at[-1].add(carried_grad * state_in)
    end_grad = end_grad.at[-1].add(carried_grad)
    sum_in_grad, size_grad_one, in_map_grad_one, log_grad_one = summary_back((span_grad, end_grad))
    pre_step_grad, dt_bias_grad = step_back(size_grad_one + size_grad_two)
    pre_step_low = pre_step_grad.astype(low_type)
    dt_proj_grad = lax.dot_general(
        rank_low, pre_step_low, rows_first, preferred_element_type=float_type
    )
    rank_grad = lax.dot_general(pre_step_low, dt_proj, last_dims, preferred_element_type=float_type)
    small_grad = jnp.concatenate(
        [rank_grad, in_map_grad_one + in_map_grad_two, out_map_grad], axis=1
    ).astype(low_type)
    x_proj_grad = lax.dot_general(
        mixer_low, small_grad, rows_first, preferred_element_type=float_type
    )
    mixer_in_grad = (
        scan_in_grad
        + sum_in_grad
        + lax.dot_general(small_grad, x_proj, last_dims, preferred_element_type=float_type)
    )
    inner_x_grad, halo_grad, conv_weight_grad, conv_bias_grad = conv_back(mixer_in_grad)
    edge_grad = shifted_2(halo_grad, "hs", -1)
    edge_total = lax.dynamic_slice_in_dim(inner_x_grad, edge_start, CONV - 1, 0) + edge_grad
    inner_x_grad = lax.dynamic_update_slice_in_dim(inner_x_grad, edge_total, edge_start, 0)
    projected_grad = jnp.concatenate([inner_x_grad, gate_pre_grad], axis=1).astype(low_type)
    in_proj_grad = lax.dot_general(
        normed_low, projected_grad, rows_first, preferred_element_type=float_type
    )
    normed_one_grad = lax.dot_general(
        projected_grad, in_proj, last_dims, preferred_element_type=float_type
    )
    tokens_norm_grad, gain_mix_grad = norm_one_back(normed_one_grad)
    tokens_grad = middle_grad + tokens_norm_grad
    gains_local = jnp.concatenate([gain_mix_grad, gain_ffn_grad])
    (
        in_proj_sum,
        conv_weight_sum,
        conv_bias_sum,
        x_proj_sum,
        dt_proj_sum,
        dt_bias_sum,
        a_log_sum,
        skip_sum,
        out_proj_sum,
        gains_sum,
        router_sum,
    ) = (
        lax.psum_scatter(in_proj_grad, ("ep", "hs"), scatter_dimension=1, tiled=True),
        lax.psum_scatter(conv_weight_grad, ("ep", "hs"), scatter_dimension=1, tiled=True),
        lax.psum_scatter(conv_bias_grad, ("ep", "hs"), scatter_dimension=0, tiled=True),
        lax.psum_scatter(x_proj_grad, ("ep", "hs"), scatter_dimension=0, tiled=True),
        lax.psum_scatter(dt_proj_grad, ("ep", "hs"), scatter_dimension=1, tiled=True),
        lax.psum_scatter(dt_bias_grad, ("ep", "hs"), scatter_dimension=0, tiled=True),
        lax.psum_scatter(
            log_grad_one + log_grad_two, ("ep", "hs"), scatter_dimension=0, tiled=True
        ),
        lax.psum_scatter(skip_grad, ("ep", "hs"), scatter_dimension=0, tiled=True),
        lax.psum_scatter(out_proj_grad, ("ep", "hs"), scatter_dimension=0, tiled=True),
        lax.psum_scatter(gains_local, ("ep", "hs"), scatter_dimension=0, tiled=True),
        lax.psum_scatter(router_grad.reshape(-1), ("ep", "hs"), scatter_dimension=0, tiled=True),
    )
    return (
        block_out,
        tokens_grad,
        gains_sum,
        router_sum,
        in_proj_sum,
        conv_weight_sum,
        conv_bias_sum,
        x_proj_sum,
        dt_proj_sum,
        dt_bias_sum,
        a_log_sum,
        skip_sum,
        out_proj_sum,
        up_grad[None],
        down_grad[None],
    )


def solution(mesh):
    return jax.shard_map(
        body,
        mesh=mesh,
        in_specs=(
            P(("ep", "hs"), None),
            P(("ep", "hs")),
            P(("ep", "hs")),
            P(("ep", "hs")),
            P(("ep", "hs")),
            P(),
            P(),
            P(),
            P(),
            P(),
            P(),
            P(),
            P(),
            P(),
            P(),
            P(),
            P(),
            P("ep", None, "hs"),
            P("ep", "hs", None),
            P(("ep", "hs"), None),
        ),
        out_specs=(
            P(("ep", "hs"), None),
            P(("ep", "hs"), None),
            P(("ep", "hs")),
            P(("ep", "hs")),
            P(None, ("ep", "hs")),
            P(None, ("ep", "hs")),
            P(("ep", "hs")),
            P(("ep", "hs"), None),
            P(None, ("ep", "hs")),
            P(("ep", "hs")),
            P(("ep", "hs"), None),
            P(("ep", "hs")),
            P(("ep", "hs"), None),
            P("ep", None, "hs"),
            P("ep", "hs", None),
        ),
        check_vma=False,
    )
```

profile of v0, /device:TPU:0, one launch (start us, length us, event | category | flops | bytes accessed | tf_op | source)
XLA Modules:
  0.0 2285.3 jit_solution(13204546932589791339)
XLA Ops:
  45.7 7.3 copy_bitcast_fusion.1
  52.9 12.8 broadcast.292.clone
  65.8 125.0 %while.107 = (s32[]{:T(128)}, f32[16,2304,16]{1,2,0:T(8,128)}, f32[16,16,2304,16]{2,3,1,0:T(8,128)}, f32[16,16,2304]{2,1,0:T(8,128)}, f32[1,2304,16]{1,2,0:T(8,1...) while((s32[]{:T(128)}, f32[16,2304,16]{1,2,0:T(8,128)}, ...), condition=%wide.region_4.5_spmd.clone, body=%wide.region_3.4_spmd.clone.sunk | while | flops 4128771 | bytes 10473276 | solution.py:121
  247.1 6.7 pad.261
  254.8 17.3 all_gather.21
  277.8 16.0 all_gather.20
  325.8 12.7 broadcast.292
  340.3 167.2 %while.105 = (s32[]{:T(128)}, f32[16,2304,16]{1,2,0:T(8,128)}, f32[16,16,2304]{2,1,0:T(8,128)}, f32[16,16,2304,16]{2,3,1,0:T(8,128)}, f32[16,16,2304]{2,1,0:T(8,...) while((s32[]{:T(128)}, f32[16,2304,16]{1,2,0:T(8,128)}, ...), condition=%wide.region_9.10_spmd, body=%wide.region_7.9_spmd.sunk | while | flops 4091906 | bytes 10919225 | solution.py:163
  518.5 15.7 all_to_all.20
  540.4 15.1 all_to_all.21
  555.8 36.4 %all-gather.4.cloned.1.call-done = bf16[32,40,1152]{2,1,0:T(8,128)(2,1)} async-done(((bf16[8,40,1152]{2,1,0:T(8,128)(2,1)}), bf16[32,40,1152]{2,1,0:T(8,128)(2,1)}) %all-gather.4.cloned.1.call-update) | async-done | bytes 2949136 | tf_op jit(solution)/shard_map/all_gather | solution.py:304
  604.4 48.3 %all-gather.6.cloned.1.call-done = bf16[32,40,1152]{2,1,0:T(8,128)(2,1)} async-done(((bf16[8,40,1152]{2,1,0:T(8,128)(2,1)}), bf16[32,40,1152]{2,1,0:T(8,128)(2,1)}) %all-gather.6.cloned.1.call-update) | async-done | bytes 2949136 | tf_op jit(solution)/shard_map/all_gather | solution.py:333
  652.7 8.2 fusion.16
  666.3 91.8 %reduce-scatter.13.cloned.1.call-done = f32[320,1152]{1,0:T(8,128)} async-done(((f32[1280,1152]{1,0:T(8,128)}), f32[320,1152]{1,0:T(8,128)}) %reduce-scatter.13.cloned.1.call-update) | async-done | bytes 1474576 | tf_op jit(solution)/shard_map/reduce_scatter | solution.py:309
  764.8 53.8 %reduce-scatter.15.cloned.1.call-done = bf16[320,1152]{1,0:T(8,128)(2,1)} async-done(((bf16[1280,1152]{1,0:T(8,128)(2,1)}), bf16[320,1152]{1,0:T(8,128)(2,1)}) %reduce-scatter.15.cloned.1.call-update) | async-done | bytes 737296 | tf_op jit(solution)/shard_map/reduce_scatter | solution.py:348
  822.9 15.0 all_gather.25
  846.3 7.7 multiply_reduce_fusion.10
  860.8 295.4 %while.109 = (s32[]{:T(128)}, f32[2304,16]{0,1:T(8,128)}, f32[16,2304,16]{1,2,0:T(8,128)}, f32[16,16,2304]{2,1,0:T(8,128)}, f32[16,16,2304]{2,1,0:T(8,128)}, /*i...) while((s32[]{:T(128)}, f32[2304,16]{0,1:T(8,128)}, ...), condition=%wide.region_24.25_spmd.clone, body=%wide.region_18.24_spmd.clone.sunk | while | flops 12938756 | bytes 22435660 | solution.py:163
  1161.1 14.4 all-gather
  1268.9 187.2 %while.110 = (s32[]{:T(128)}, f32[2304,16]{0,1:T(8,128)}, f32[16,2304,16]{1,2,0:T(8,128)S(1)}, f32[16,16,2304]{2,1,0:T(8,128)}, f32[16,16,2304]{2,1,0:T(8,128)},...) while((s32[]{:T(128)}, f32[2304,16]{0,1:T(8,128)}, ...), condition=%wide.region_33.34_spmd.clone, body=%wide.region_28.33_spmd.clone.sunk | while | flops 8220420 | bytes 14316927 | solution.py:121
  1460.1 6.7 pad.309
  1492.9 9.0 fusion.121
  1506.7 8.5 multiply_reduce_fusion.15
  1530.4 9.7 fusion.50
  1545.9 7.0 fusion.115
  1554.4 11.7 fusion.45
  1566.1 6.9 convolution_bitcast_fusion.1
  1579.4 86.1 %all-reduce.74.cloned.1.call-done = (f32[2304]{0:T(1024)}, f32[9216]{0:T(1024)}, f32[4,2304]{1,0:T(4,128)}, f32[2304]{0:T(1024)}, f32[2304]{0:T(1024)}, /*index=5*/f32[2304]{0:T(1024)}) async-done(((f32[2304]{0:T(1024)}, f32[9216]{0:T(1024)}, f32[4,2304]{1,0:T(4,128)}, f32[2304]{0:T(1024)}, f32[2304]{0:T(1024)}, /*index=5*/f32[2304]{0:T(1024)}), (f32[2304]{0:T(1024)}, f32[9216]{0:T(1024)}, ...) | async-done | bytes 110608
  1673.3 126.4 %all-reduce.76.cloned.1.call-done = (f32[72,2304]{1,0:T(8,128)}, f32[2304,16]{0,1:T(8,128)}) async-done(((f32[72,2304]{1,0:T(8,128)}, f32[2304,16]{0,1:T(8,128)}), (f32[72,2304]{1,0:T(8,128)}, f32[2304,16]{0,1:T(8,128)})) %all-reduce.76.cloned.1.call-update) | async-done | bytes 811024
  1802.6 100.1 %reduce-scatter.19.cloned.1.call-done = f32[72,104]{1,0:T(8,128)} async-done(((f32[2304,104]{1,0:T(8,128)}), f32[72,104]{1,0:T(8,128)}) %reduce-scatter.19.cloned.1.call-update) | async-done | bytes 29968
  1902.7 148.7 %reduce-scatter.21.cloned.1.call-done = f32[72,1152]{1,0:T(8,128)} async-done(((f32[2304,1152]{1,0:T(8,128)}), f32[72,1152]{1,0:T(8,128)}) %reduce-scatter.21.cloned.1.call-update) | async-done | bytes 331792
  2051.4 227.0 %reduce-scatter.17.cloned.1.call-done = f32[1152,144]{0,1:T(8,128)} async-done(((f32[1152,4608]{0,1:T(8,128)}), f32[1152,144]{0,1:T(8,128)}) %reduce-scatter.17.cloned.1.call-update) | async-done | bytes 663568 | tf_op jit(solution)/shard_map/reduce_scatter | solution.py:437
  (1275 shorter events, 1145.6 us)
Async XLA Ops:
  7.2 592.0 %copy-start = (bf16[1,768,1152]{2,1,0:T(8,128)(2,1)S(1)}, bf16[1,768,1152]{2,1,0:T(8,128)(2,1)}, u32[]{:S(2)}) copy-start(bf16[1,768,1152]{2,1,0:T(8,128)(2,1)} %param.54) | copy-start | bytes 5308420
  7.2 585.0 %all-gather.4.cloned.1.call-start = ((), (), s32[]{:S(2)}) async-start(), calls=%async_computation.9 | async-start | bytes 3686400 | tf_op jit(solution)/shard_map/all_gather | solution.py:304
  20.7 11.0 collective-permute-start
  25.8 5.5 collective-permute-start.1
  31.7 159.1 %copy-start.145 = (f32[16]{0:T(128)}, f32[16]{0:T(128)S(1)}, u32[]{:S(2)}) copy-start(f32[16]{0:T(128)S(1)} %reduce_prod.9) | copy-start | bytes 196
  43.2 147.6 %copy-start.88 = (f32[16,2304]{1,0:T(8,128)}, f32[16,2304]{1,0:T(8,128)S(1)}, u32[]{:S(2)}) copy-start(f32[16,2304]{1,0:T(8,128)S(1)} %get-tuple-element.1287) | copy-start | bytes 442372
  217.9 15.9 copy-start.13
  297.2 26.5 %copy-start.42 = (f32[2304,16]{0,1:T(8,128)}, f32[2304,16]{0,1:T(8,128)S(1)}, u32[]{:S(2)}) copy-start(f32[2304,16]{0,1:T(8,128)S(1)} %get-tuple-element.867) | copy-start | bytes 442372
  517.9 20.7 copy-start.55
  534.2 118.5 %all-gather.6.cloned.1.call-start = ((), (), s32[]{:S(2)}) async-start(), calls=%async_computation.11 | async-start | bytes 3686400 | tf_op jit(solution)/shard_map/all_gather | solution.py:333
  536.2 303.3 %copy-start.99 = (f32[256,8]{0,1:T(8,128)}, f32[256,8]{0,1:T(8,128)S(1)}, u32[]{:S(2)}) copy-start(f32[256,8]{0,1:T(8,128)S(1)} %get-tuple-element.1369) | copy-start | bytes 24580
  555.6 202.5 %reduce-scatter.13.cloned.1.call-start = ((), (), s32[]{:S(2)}) async-start(), calls=%async_computation.10 | async-start | bytes 7372800 | tf_op jit(solution)/shard_map/reduce_scatter | solution.py:309
  604.4 214.2 %reduce-scatter.15.cloned.1.call-start = ((), (), s32[]{:S(2)}) async-start(), calls=%async_computation.12 | async-start | bytes 3686400 | tf_op jit(solution)/shard_map/reduce_scatter | solution.py:348
  666.3 156.6 %copy-start.96 = (bf16[1,2304,16]{1,2,0:T(8,128)(2,1)S(1)}, bf16[1,2304,16]{1,2,0:T(8,128)(2,1)}, u32[]{:S(2)}) copy-start(bf16[1,2304,16]{1,2,0:T(8,128)(2,1)} %get-tuple-element.1285) | copy-start | bytes 221188
  666.3 171.6 %copy-start.120 = (s32[256]{0:T(256)S(1)}, s32[256]{0:T(256)}, u32[]{:S(2)}) copy-start(s32[256]{0:T(256)} %multiply_add_fusion.11) | copy-start | bytes 3076
  666.3 171.6 %copy-start.142 = (pred[256]{0:T(512)(128)(4,1)S(1)}, pred[256]{0:T(512)(128)(4,1)}, u32[]{:S(2)}) copy-start(pred[256]{0:T(512)(128)(4,1)} %broadcast_compare_fusion) | copy-start | bytes 772
  760.4 58.2 %all-to-all-start.1 = ((bf16[8,40,1152]{2,1,0:T(8,128)(2,1)}), bf16[8,40,1152]{2,1,0:T(8,128)(2,1)S(1)}, u32[]{:S(2)}, u32[]{:S(2)}) async-start(bf16[8,40,1152]{2,1,0:T(8,128)(2,1)} %bitcast.25), calls=%async_computation.2 | async-start | bytes 1474560 | tf_op jit(solution)/shard_map/all_to_all | solution.py:310
  764.1 75.4 %copy-start.101 = (f32[1152,8]{0,1:T(8,128)S(1)}, f32[1152,8]{0,1:T(8,128)}, u32[]{:S(2)}) copy-start(f32[1152,8]{0,1:T(8,128)} %param.52) | copy-start | bytes 110596
  764.1 75.4 %copy-start.122 = (f32[256]{0:T(256)S(1)}, f32[256]{0:T(256)}, u32[]{:S(2)}) copy-start(f32[256]{0:T(256)} %copy-done.121) | copy-start | bytes 3076
  764.1 75.4 %copy-start.125 = (f32[256]{0:T(256)S(1)}, f32[256]{0:T(256)}, u32[]{:S(2)}) copy-start(f32[256]{0:T(256)} %copy-done.124) | copy-start | bytes 3076
  764.1 75.4 %copy-start.128 = (s32[256]{0:T(256)S(1)}, s32[256]{0:T(256)}, u32[]{:S(2)}) copy-start(s32[256]{0:T(256)} %param.39) | copy-start | bytes 3076
  764.1 75.4 %copy-start.131 = (f32[256]{0:T(256)S(1)}, f32[256]{0:T(256)}, u32[]{:S(2)}) copy-start(f32[256]{0:T(256)} %copy-done.130) | copy-start | bytes 3076
  818.6 22.1 all-to-all-start.3
  822.8 17.9 copy-start.114
  822.9 842.6 %all-reduce.74.cloned.1.call-start = ((), (), s32[]{:S(2)}) async-start(), calls=%async_computation.16 | async-start | bytes 245760
  1161.1 19.5 copy-start.24
  1516.3 9.7 collective-permute-start.2
  1540.7 258.9 %all-reduce.76.cloned.1.call-start = ((), (), s32[]{:S(2)}) async-start(), calls=%async_computation.17 | async-start | bytes 1622016
  1542.9 359.8 %reduce-scatter.19.cloned.1.call-start = ((), (), s32[]{:S(2)}) async-start(), calls=%async_computation.14 | async-start | bytes 1216512
  1545.9 505.5 %reduce-scatter.21.cloned.1.call-start = ((), (), s32[]{:S(2)}) async-start(), calls=%async_computation.15 | async-start | bytes 10948608
  1552.9 725.4 %reduce-scatter.17.cloned.1.call-start = ((), (), s32[]{:S(2)}) async-start(), calls=%async_computation.13 | async-start | bytes 21897216 | tf_op jit(solution)/shard_map/reduce_scatter | solution.py:437
  1573.1 705.3 %copy-start.1 = (bf16[1,768,1152]{2,1,0:T(8,128)(2,1)S(1)}, bf16[1,768,1152]{2,1,0:T(8,128)(2,1)}, u32[]{:S(2)}) copy-start(bf16[1,768,1152]{2,1,0:T(8,128)(2,1)} %param.54) | copy-start | bytes 5308420
  (241 other events, 764.7 us)
Sparse Core Ops, SparseCore 0:
  534.3 57.8 all-gather.3
  593.7 58.9 all-gather.5
  655.0 103.0 reduce-scatter.12
  760.8 57.7 reduce-scatter.14
  1540.8 124.5 all-reduce.73
  1671.4 128.1 all-reduce.75
  1806.1 96.5 reduce-scatter.18
  1910.4 140.9 reduce-scatter.20
  2059.5 218.7 reduce-scatter.16
where the time goes:
time: 2310 us; the launch traced here: 2290 us
  waiting for transfers between devices  919 us (40%)
  local copies, waits for them, and re-layouts  644 us (28%)
  other arithmetic  481 us (21%)
  matrix products  110 us (5%)
  blocking collectives  93.5 us (4%)
    unnamed x13, waiting for transfers between devices  461 us
    reduce_scatter x1, waiting for transfers between devices, body(): lax.psum_scatter(in_proj_grad, ('ep', 'hs'), scatter_dimension=1, tiled=T...  227 us
    squeeze x160, local copies, waits for them, and re-layouts, block_summaries(): block_ends, _ = lax.scan(jax.checkpoint(advance), initial, sequence)  170 us
    reduce_sum x32, other arithmetic, advance(): stride[:, :, None] * rate_table[None]  134 us
    pad x31, local copies, waits for them, and re-layouts, block_summaries(): return lax.associative_scan(join_forward, (block_spans, block_ends), axis=0)  107 us
    reduce_scatter x1, waiting for transfers between devices, body(): lax.psum_scatter(partial_out, 'hs', scatter_dimension=0, tiled=True)  91.8 us
    reduce_sum x16, other arithmetic, advance(): return (memory, jnp.sum(memory * out_map[:, None, :], axis=2))  65.9 us
    dynamic_update_slice x96, local copies, waits for them, and re-layouts, block_outputs(): _, readout = lax.scan(jax.checkpoint(advance), opening, sequence)  62.7 us
  transfers between devices with their start and end apart: 14, of which 9 were waited for; matrix products, arithmetic and copies ran while one was open for 4% of the time, Pallas kernels for 0%

commit v1 on v0

v1 whole, which is shorter than its diff:
```python
import jax
import jax.numpy as jnp
from jax import lax
from jax.experimental import pallas as pl
from jax.experimental.pallas import tpu as pltpu
from jax.sharding import PartitionSpec as P

DT_RANK = 72
CONV = 4
STATE = 16
SEGMENTS = 8
LANES = 128
RESET = 1e30
LN2 = 0.6931471805599453


def spread_columns(target, source, staging, steps):
    rows = source.shape[0]
    for n in range(STATE):
        staging[...] = jnp.broadcast_to(source[:, n : n + 1], (rows, LANES))

        @pl.loop(0, steps)
        def _(i, n=n):
            target[i, n] = staging[pl.ds(i, SEGMENTS, stride=steps), :]


def spread_flags(target, source, staging, steps):
    staging[...] = jnp.broadcast_to(source[...] * RESET, (source.shape[0], LANES))

    @pl.loop(0, steps)
    def _(i):
        target[i] = staging[pl.ds(i, SEGMENTS, stride=steps), :]


def spread_rates(target, rates):
    for n in range(STATE):
        target[n] = jnp.broadcast_to(rates[n : n + 1, :], (SEGMENTS, LANES))


def ends_kernel(x, dt, in_map, starts, rates, ends_ex, cum_ex, end_all, cum_all,
                in_wide, big, staging, rate_wide, end_scr, sum_scr):
    steps = x.shape[0] // SEGMENTS

    @pl.when(pl.program_id(0) == 0)
    def _():
        spread_columns(in_wide, in_map, staging, steps)
        spread_flags(big, starts, staging, steps)

    spread_rates(rate_wide, rates)

    def step(i, carry):
        total, states = carry[0], carry[1:]
        rows = pl.ds(i, SEGMENTS, stride=steps)
        stride = dt[rows, :]
        driven = stride * x[rows, :]
        stride = stride + big[i]
        new = [total + stride]
        for n in range(STATE):
            new.append(jnp.exp2(stride * rate_wide[n]) * states[n] + driven * in_wide[i, n])
        return tuple(new)

    zero = jnp.zeros((SEGMENTS, LANES), jnp.float32)
    done = lax.fori_loop(0, steps, step, (zero,) * (STATE + 1), unroll=2)
    sum_scr[...] = done[0]
    for n in range(STATE):
        end_scr[n * SEGMENTS : (n + 1) * SEGMENTS, :] = done[1 + n]
    state = jnp.zeros((STATE, LANES), jnp.float32)
    cum = jnp.zeros((1, LANES), jnp.float32)
    for s in range(SEGMENTS):
        ends_ex[s * STATE : (s + 1) * STATE, :] = state
        cum_ex[s : s + 1, :] = cum
        own = sum_scr[s : s + 1, :]
        state = jnp.exp2(own * rates[...]) * state + end_scr[pl.ds(s, STATE, stride=SEGMENTS), :]
        cum = cum + own
    end_all[...] = state
    cum_all[...] = cum


def outputs_kernel(x, dt, in_map, out_map, starts, rates, ends_ex, cum_ex, entering, skip, gate,
                   scan_out, gated, in_wide, out_wide, big, staging, rate_wide):
    steps = x.shape[0] // SEGMENTS

    @pl.when(pl.program_id(0) == 0)
    def _():
        spread_columns(in_wide, in_map, staging, steps)
        spread_columns(out_wide, out_map, staging, steps)
        spread_flags(big, starts, staging, steps)

    spread_rates(rate_wide, rates)
    cum = cum_ex[...]
    opening = tuple(
        jnp.exp2(cum * rate_wide[n]) * entering[n : n + 1, :]
        + ends_ex[pl.ds(n, SEGMENTS, stride=STATE), :]
        for n in range(STATE)
    )

    def step(i, states):
        rows = pl.ds(i, SEGMENTS, stride=steps)
        stride = dt[rows, :]
        driven = stride * x[rows, :]
        stride = stride + big[i]
        new, total = [], None
        for n in range(STATE):
            state = jnp.exp2(stride * rate_wide[n]) * states[n] + driven * in_wide[i, n]
            new.append(state)
            term = state * out_wide[i, n]
            total = term if total is None else total + term
        scan_out[rows, :] = total
        return tuple(new)

    lax.fori_loop(0, steps, step, opening, unroll=2)
    value = scan_out[...] + skip[...] * x[...]
    scan_out[...] = value
    gated[...] = (value * jax.nn.silu(gate[...])).astype(gated.dtype)


def adjoint_kernel(gated_grad, gate, scan_out, dt, out_map, starts, rates,
                   scan_grad, gate_grad, adj_ex, cum_ex, adj_all,
                   out_wide, big, staging, rate_wide, end_scr, sum_scr):
    steps = dt.shape[0] // SEGMENTS

    @pl.when(pl.program_id(0) == 0)
    def _():
        spread_columns(out_wide, out_map, staging, steps)
        spread_flags(big, starts, staging, steps)

    spread_rates(rate_wide, rates)
    incoming = gated_grad[...]
    gate_in = gate[...]
    chance = jax.nn.sigmoid(gate_in)
    scan_grad[...] = incoming * (gate_in * chance)
    gate_grad[...] = (
        incoming * scan_out[...] * (chance * (1.0 + gate_in * (1.0 - chance)))
    ).astype(gate_grad.dtype)

    def step(k, carry):
        i = steps - 1 - k
        total, tails = carry[0], carry[1:]
        rows = pl.ds(i, SEGMENTS, stride=steps)
        grad = scan_grad[rows, :]
        stride = dt[rows, :] + big[i]
        new = [total + stride]
        for n in range(STATE):
            new.append(jnp.exp2(stride * rate_wide[n]) * (grad * out_wide[i, n] + tails[n]))
        return tuple(new)

    zero = jnp.zeros((SEGMENTS, LANES), jnp.float32)
    done = lax.fori_loop(0, steps, step, (zero,) * (STATE + 1), unroll=2)
    sum_scr[...] = done[0]
    for n in range(STATE):
        end_scr[n * SEGMENTS : (n + 1) * SEGMENTS, :] = done[1 + n]
    tail = jnp.zeros((STATE, LANES), jnp.float32)
    cum = jnp.zeros((1, LANES), jnp.float32)
    for s in reversed(range(SEGMENTS)):
        adj_ex[s * STATE : (s + 1) * STATE, :] = tail
        cum_ex[s : s + 1, :] = cum
        own = sum_scr[s : s + 1, :]
        tail = jnp.exp2(own * rates[...]) * tail + end_scr[pl.ds(s, STATE, stride=SEGMENTS), :]
        cum = cum + own
    adj_all[...] = tail


def grads_kernel(x, dt, in_map, out_map, starts, rates, ends_ex, cum_ex, entering, skip,
                 scan_grad, adj_ex, back_cum_ex, returning,
                 x_grad, dt_grad, in_grad, out_grad, log_grad, skip_grad,
                 in_wide, out_wide, big, staging, rate_wide, kept, log_scr):
    steps = x.shape[0] // SEGMENTS

    @pl.when(pl.program_id(0) == 0)
    def _():
        spread_columns(in_wide, in_map, staging, steps)
        spread_columns(out_wide, out_map, staging, steps)
        spread_flags(big, starts, staging, steps)
        in_grad[...] = jnp.zeros_like(in_grad)
        out_grad[...] = jnp.zeros_like(out_grad)

    spread_rates(rate_wide, rates)
    cum = cum_ex[...]
    opening = tuple(
        jnp.exp2(cum * rate_wide[n]) * entering[n : n + 1, :]
        + ends_ex[pl.ds(n, SEGMENTS, stride=STATE), :]
        for n in range(STATE)
    )

    def forward(i, states):
        rows = pl.ds(i, SEGMENTS, stride=steps)
        stride = dt[rows, :]
        driven = stride * x[rows, :]
        stride = stride + big[i]
        new = []
        for n in range(STATE):
            remain = jnp.exp2(stride * rate_wide[n]) * states[n]
            kept[i, n] = remain
            new.append(remain + driven * in_wide[i, n])
        return tuple(new)

    lax.fori_loop(0, steps, forward, opening, unroll=2)

    back_cum = back_cum_ex[...]
    tails = tuple(
        jnp.exp2(back_cum * rate_wide[n]) * returning[n : n + 1, :]
        + adj_ex[pl.ds(n, SEGMENTS, stride=STATE), :]
        for n in range(STATE)
    )
    zero = jnp.zeros((SEGMENTS, LANES), jnp.float32)
    for n in range(STATE):
        log_scr[n] = zero

    def backward(k, tails):
        i = steps - 1 - k
        rows = pl.ds(i, SEGMENTS, stride=steps)
        stride = dt[rows, :]
        value = x[rows, :]
        driven = stride * value
        grad = scan_grad[rows, :]
        marked = stride + big[i]
        new = []
        drive_sum, rate_sum = None, None
        for n in range(STATE):
            rate = rate_wide[n]
            in_n = in_wide[i, n]
            adjoint = grad * out_wide[i, n] + tails[n]
            remain = kept[i, n]
            out_grad[i, n] += grad * (remain + driven * in_n)
            in_grad[i, n] += adjoint * driven
            drive = adjoint * in_n
            touched = adjoint * remain
            slope = touched * rate
            log_scr[n] += touched * stride
            drive_sum = drive if drive_sum is None else drive_sum + drive
            rate_sum = slope if rate_sum is None else rate_sum + slope
            new.append(jnp.exp2(marked * rate) * adjoint)
        x_grad[rows, :] = stride * drive_sum
        dt_grad[rows, :] = value * drive_sum + LN2 * rate_sum
        return tuple(new)

    lax.fori_loop(0, steps, backward, tails)
    for n in range(STATE):
        log_grad[n : n + 1, :] = (
            jnp.sum(log_scr[n], axis=0, keepdims=True) * rates[n : n + 1, :] * LN2
        )
    skip_grad[...] = jnp.sum(scan_grad[...] * x[...], axis=0, keepdims=True)
    x_grad[...] += skip[...] * scan_grad[...]


def tile(rows):
    return pl.BlockSpec((rows, LANES), lambda j: (0, j))


def whole(shape):
    return pl.BlockSpec(shape, lambda j: (0,) * len(shape))


def shape_of(rows, width, dtype=jnp.float32):
    return jax.ShapeDtypeStruct((rows, width), dtype)


PARAMS = pltpu.CompilerParams(
    dimension_semantics=("arbitrary",), vmem_limit_bytes=56 * 1024 * 1024
)
WIDE = lambda steps: pltpu.VMEM((steps, STATE, SEGMENTS, LANES), jnp.float32)
FLAG = lambda steps: pltpu.VMEM((steps, SEGMENTS, LANES), jnp.float32)
BLOCK = lambda rows: pltpu.VMEM((rows, LANES), jnp.float32)
RATE = pltpu.VMEM((STATE, SEGMENTS, LANES), jnp.float32)


def scan_ends(x, dt, in_map, starts, rates):
    rows, width = x.shape
    steps = rows // SEGMENTS
    return pl.pallas_call(
        ends_kernel,
        grid=(width // LANES,),
        in_specs=[tile(rows), tile(rows), whole((rows, STATE)), whole((rows, 1)), tile(STATE)],
        out_specs=[tile(SEGMENTS * STATE), tile(SEGMENTS), tile(STATE), tile(1)],
        out_shape=[shape_of(SEGMENTS * STATE, width), shape_of(SEGMENTS, width),
                   shape_of(STATE, width), shape_of(1, width)],
        scratch_shapes=[WIDE(steps), FLAG(steps), BLOCK(rows), RATE, BLOCK(SEGMENTS * STATE),
                        BLOCK(SEGMENTS)],
        compiler_params=PARAMS, name="scan_ends",
    )(x, dt, in_map, starts, rates)


def scan_outputs(x, dt, in_map, out_map, starts, rates, ends_ex, cum_ex, entering, skip, gate):
    rows, width = x.shape
    steps = rows // SEGMENTS
    return pl.pallas_call(
        outputs_kernel,
        grid=(width // LANES,),
        in_specs=[tile(rows), tile(rows), whole((rows, STATE)), whole((rows, STATE)),
                  whole((rows, 1)), tile(STATE), tile(SEGMENTS * STATE), tile(SEGMENTS),
                  tile(STATE), tile(1), tile(rows)],
        out_specs=[tile(rows), tile(rows)],
        out_shape=[shape_of(rows, width), shape_of(rows, width, jnp.bfloat16)],
        scratch_shapes=[WIDE(steps), WIDE(steps), FLAG(steps), BLOCK(rows), RATE],
        compiler_params=PARAMS, name="scan_outputs",
    )(x, dt, in_map, out_map, starts, rates, ends_ex, cum_ex, entering, skip, gate)


def scan_adjoints(gated_grad, gate, scan_out, dt, out_map, starts, rates):
    rows, width = dt.shape
    steps = rows // SEGMENTS
    return pl.pallas_call(
        adjoint_kernel,
        grid=(width // LANES,),
        in_specs=[tile(rows), tile(rows), tile(rows), tile(rows), whole((rows, STATE)),
                  whole((rows, 1)), tile(STATE)],
        out_specs=[tile(rows), tile(rows), tile(SEGMENTS * STATE), tile(SEGMENTS), tile(STATE)],
        out_shape=[shape_of(rows, width), shape_of(rows, width, jnp.bfloat16),
                   shape_of(SEGMENTS * STATE, width), shape_of(SEGMENTS, width),
                   shape_of(STATE, width)],
        scratch_shapes=[WIDE(steps), FLAG(steps), BLOCK(rows), RATE, BLOCK(SEGMENTS * STATE),
                        BLOCK(SEGMENTS)],
        compiler_params=PARAMS, name="scan_adjoints",
    )(gated_grad, gate, scan_out, dt, out_map, starts, rates)


def scan_grads(x, dt, in_map, out_map, starts, rates, ends_ex, cum_ex, entering, skip,
               scan_grad, adj_ex, back_cum_ex, returning):
    rows, width = x.shape
    steps = rows // SEGMENTS
    wide_shape = (steps, STATE, SEGMENTS, LANES)
    return pl.pallas_call(
        grads_kernel,
        grid=(width // LANES,),
        in_specs=[tile(rows), tile(rows), whole((rows, STATE)), whole((rows, STATE)),
                  whole((rows, 1)), tile(STATE), tile(SEGMENTS * STATE), tile(SEGMENTS),
                  tile(STATE), tile(1), tile(rows), tile(SEGMENTS * STATE), tile(SEGMENTS),
                  tile(STATE)],
        out_specs=[tile(rows), tile(rows), whole(wide_shape), whole(wide_shape), tile(STATE),
                   tile(1)],
        out_shape=[shape_of(rows, width), shape_of(rows, width),
                   jax.ShapeDtypeStruct(wide_shape, jnp.float32),
                   jax.ShapeDtypeStruct(wide_shape, jnp.float32),
                   shape_of(STATE, width), shape_of(1, width)],
        scratch_shapes=[WIDE(steps), WIDE(steps), FLAG(steps), BLOCK(rows), RATE, WIDE(steps),
                        RATE],
        compiler_params=PARAMS, name="scan_grads",
    )(x, dt, in_map, out_map, starts, rates, ends_ex, cum_ex, entering, skip, scan_grad, adj_ex,
      back_cum_ex, returning)


def fold_map(wide):
    summed = jnp.sum(wide, axis=3)
    return jnp.transpose(summed, (2, 0, 1)).reshape(-1, STATE)


norm_epsilon = 1e-05
highest = lax.Precision.HIGHEST


def shifted_2(block, axis, distance):
    devices = range(lax.axis_size(axis))
    route = [(i - distance, i) for i in devices if i - distance in devices]
    return lax.ppermute(block, axis, route)


def state_before(cum, end, rates, axis):
    count, mine = lax.axis_size(axis), lax.axis_index(axis)
    cums = lax.all_gather(cum, axis)
    ends = lax.all_gather(end.astype(jnp.bfloat16), axis).astype(jnp.float32)
    state = jnp.zeros_like(end)
    for d in range(count - 1):
        state = jnp.where(d < mine, jnp.exp2(cums[d] * rates) * state + ends[d], state)
    return state, cums


def state_after(cums, tail, rates, axis):
    count, mine = lax.axis_size(axis), lax.axis_index(axis)
    tails = lax.all_gather(tail.astype(jnp.bfloat16), axis).astype(jnp.float32)
    state = jnp.zeros_like(tail)
    for d in reversed(range(1, count)):
        state = jnp.where(d > mine, jnp.exp2(cums[d] * rates) * state + tails[d], state)
    return state


def rms_scale(values):
    return lax.rsqrt(jnp.mean(values * values, axis=1, keepdims=True) + norm_epsilon)


def scaled_norm(values, gain_row):
    return values * rms_scale(values) * gain_row[None, :]


def gelu_tanh(values):
    return jax.nn.gelu(values, approximate=True)


def conv_mix(x_inner, halo_rows, halo_flags, start_flags, conv_w, conv_b):
    tap_count = conv_w.shape[0]
    length = x_inner.shape[0]
    extended = jnp.concatenate([halo_rows, x_inner], axis=0)
    flag_line = jnp.concatenate([halo_flags, start_flags], axis=0)
    result = conv_b[None, :] + conv_w[tap_count - 1][None, :] * x_inner
    survive = jnp.ones((length,), jnp.float32)
    for offset in range(1, tap_count):
        survive = survive * (1.0 - flag_line[tap_count - offset : tap_count - offset + length])
        shifted = extended[tap_count - 1 - offset : tap_count - 1 - offset + length]
        result = result + conv_w[tap_count - 1 - offset][None, :] * shifted * survive[:, None]
    return jax.nn.silu(result)


def delta_apply(step_pre, bias_row, real_rows):
    return jax.nn.softplus(step_pre + bias_row[None, :]) * real_rows[:, None]


def body(
    tokens,
    starts,
    counts,
    routes,
    slot_index,
    gain_mix,
    in_proj,
    conv_weight,
    conv_bias,
    x_proj,
    dt_proj,
    dt_bias,
    a_log,
    skip_gain,
    out_proj,
    gain_ffn,
    router,
    up_proj,
    down_proj,
    out_grad,
):
    float_type = jnp.float32
    low_type = jnp.bfloat16
    rows_first = (((0,), (0,)), ((), ()))
    last_dims = (((1,), (1,)), ((), ()))
    length = tokens.shape[0]
    model_width = tokens.shape[1]
    inner_width = conv_bias.shape[0]
    experts = router.shape[1]
    capacity = 5 * length // (4 * experts)
    edge_start = counts[0] - (CONV - 1)
    start_flags = starts.astype(float_type)
    real_rows = (jnp.arange(length, dtype=jnp.int32) < counts[0]).astype(float_type)
    tokens_float = tokens.astype(float_type)
    normed_one, norm_one_back = jax.vjp(scaled_norm, tokens_float, gain_mix)
    normed_low = normed_one.astype(low_type)
    projected = jnp.dot(normed_low, in_proj, preferred_element_type=float_type)
    inner_x = projected[:, :inner_width]
    inner_gate = projected[:, inner_width:]
    edge_rows = lax.dynamic_slice_in_dim(inner_x, edge_start, CONV - 1, 0)
    edge_flags = lax.dynamic_slice_in_dim(start_flags, edge_start, CONV - 1, 0)
    halo_rows, halo_flags = shifted_2((edge_rows, edge_flags), "hs", 1)

    def conv_part(x_part, rows_part, weight_part, bias_part):
        return conv_mix(x_part, rows_part, halo_flags, start_flags, weight_part, bias_part)

    mixer_in, conv_back = jax.vjp(conv_part, inner_x, halo_rows, conv_weight, conv_bias)
    mixer_low = mixer_in.astype(low_type)
    small_proj = jnp.dot(mixer_low, x_proj, preferred_element_type=float_type)
    rank_low = small_proj[:, :DT_RANK].astype(low_type)
    step_pre = jnp.dot(rank_low, dt_proj, preferred_element_type=float_type)
    input_map = small_proj[:, DT_RANK : DT_RANK + STATE]
    output_map = small_proj[:, DT_RANK + STATE :]

    def step_part(pre_part, bias_part):
        return delta_apply(pre_part, bias_part, real_rows)

    step_size, step_back = jax.vjp(step_part, step_pre, dt_bias)

    start_column = start_flags[:, None]
    rates = -(jnp.exp(a_log) / LN2).T
    skip_row = skip_gain[None, :]
    ends_ex, cum_ex, end_all, cum_all = scan_ends(
        mixer_in, step_size, input_map, start_column, rates
    )
    entering, cums = state_before(cum_all, end_all, rates, "hs")
    scan_out, gated_low = scan_outputs(
        mixer_in,
        step_size,
        input_map,
        output_map,
        start_column,
        rates,
        ends_ex,
        cum_ex,
        entering,
        skip_row,
        inner_gate,
    )
    mixer_out = jnp.dot(gated_low, out_proj, preferred_element_type=float_type)
    middle = tokens_float + mixer_out * real_rows[:, None]
    normed_two, norm_two_back = jax.vjp(scaled_norm, middle, gain_ffn)
    router_probs = jax.nn.softmax(
        jnp.dot(normed_two, router, precision=highest, preferred_element_type=float_type), axis=1
    )
    chosen = (routes[:, None] == jnp.arange(experts, dtype=jnp.int32)[None, :]).astype(float_type)
    gate_value = jnp.sum(router_probs * chosen, axis=1)
    column = routes * capacity + slot_index
    placed = (
        (column[:, None] == jnp.arange(experts * capacity, dtype=jnp.int32)[None, :])
        & (slot_index[:, None] >= 0)
    ).astype(low_type)
    dispatched = lax.dot_general(
        placed, normed_two.astype(low_type), rows_first, preferred_element_type=float_type
    ).astype(low_type)
    arrived = lax.all_to_all(
        dispatched.reshape(experts, capacity, model_width),
        "ep",
        split_axis=0,
        concat_axis=0,
        tiled=True,
    )
    gathered_rows = lax.all_gather(arrived, "hs", axis=0, tiled=True).reshape(-1, model_width)
    hidden_pre = jnp.dot(gathered_rows, up_proj[0], preferred_element_type=float_type)
    hidden, gelu_back = jax.vjp(gelu_tanh, hidden_pre)
    hidden_low = hidden.astype(low_type)
    partial_out = jnp.dot(hidden_low, down_proj[0], preferred_element_type=float_type)
    returned = lax.psum_scatter(partial_out, "hs", scatter_dimension=0, tiled=True).astype(low_type)
    home_rows = lax.all_to_all(
        returned.reshape(-1, capacity, model_width), "ep", split_axis=0, concat_axis=0, tiled=True
    )
    expert_out = jnp.dot(
        placed,
        home_rows.reshape(experts * capacity, model_width),
        preferred_element_type=float_type,
    )
    block_out = (middle + gate_value[:, None] * expert_out).astype(low_type)
    grad_out = out_grad.astype(float_type)
    gate_grad = jnp.sum(grad_out * expert_out, axis=1)
    token_grad = grad_out * gate_value[:, None]
    placed_full = placed.astype(float_type)
    rows_grad = lax.dot_general(
        placed_full, token_grad, rows_first, precision=highest, preferred_element_type=float_type
    ).astype(low_type)
    arrived_grad = lax.all_to_all(
        rows_grad.reshape(experts, capacity, model_width),
        "ep",
        split_axis=0,
        concat_axis=0,
        tiled=True,
    )
    gathered_grad = lax.all_gather(arrived_grad, "hs", axis=0, tiled=True).reshape(-1, model_width)
    hidden_grad = lax.dot_general(
        gathered_grad, down_proj[0], last_dims, preferred_element_type=float_type
    )
    down_grad = lax.dot_general(
        hidden_low, gathered_grad, rows_first, preferred_element_type=float_type
    )
    pre_grad = gelu_back(hidden_grad)[0].astype(low_type)
    up_grad = lax.dot_general(
        gathered_rows, pre_grad, rows_first, preferred_element_type=float_type
    )
    partial_grad = lax.dot_general(
        pre_grad, up_proj[0], last_dims, preferred_element_type=float_type
    )
    own_grad = (
        lax.psum_scatter(partial_grad.astype(jnp.bfloat16), "hs", scatter_dimension=0, tiled=True)
        .astype(jnp.float32)
        .astype(low_type)
    )
    home_grad = lax.all_to_all(
        own_grad.reshape(-1, capacity, model_width), "ep", split_axis=0, concat_axis=0, tiled=True
    )
    normed_two_grad = jnp.dot(
        placed_full,
        home_grad.reshape(experts * capacity, model_width).astype(float_type),
        precision=highest,
        preferred_element_type=float_type,
    )
    logit_grad = router_probs * gate_grad[:, None] * (chosen - gate_value[:, None])
    router_grad = lax.dot_general(
        normed_two, logit_grad, rows_first, precision=highest, preferred_element_type=float_type
    )
    normed_two_grad = normed_two_grad + lax.dot_general(
        logit_grad, router, last_dims, precision=highest, preferred_element_type=float_type
    )
    middle_norm_grad, gain_ffn_grad = norm_two_back(normed_two_grad)
    middle_grad = grad_out + middle_norm_grad
    mixer_grad = (middle_grad * real_rows[:, None]).astype(low_type)
    out_proj_grad = lax.dot_general(
        gated_low, mixer_grad, rows_first, preferred_element_type=float_type
    )
    gated_grad = lax.dot_general(mixer_grad, out_proj, last_dims, preferred_element_type=float_type)
    scan_grad, gate_pre_low, adj_ex, back_cum_ex, adj_all = scan_adjoints(
        gated_grad, inner_gate, scan_out, step_size, output_map, start_column, rates
    )
    returning = state_after(cums, adj_all, rates, "hs")
    scan_in_grad, size_grad, in_wide_grad, out_wide_grad, log_grad, skip_grad = scan_grads(
        mixer_in,
        step_size,
        input_map,
        output_map,
        start_column,
        rates,
        ends_ex,
        cum_ex,
        entering,
        skip_row,
        scan_grad,
        adj_ex,
        back_cum_ex,
        returning,
    )
    pre_step_grad, dt_bias_grad = step_back(size_grad)
    pre_step_low = pre_step_grad.astype(low_type)
    dt_proj_grad = lax.dot_general(
        pre_step_low, rank_low, rows_first, preferred_element_type=float_type
    )
    rank_grad = lax.dot_general(pre_step_low, dt_proj, last_dims, preferred_element_type=float_type)
    small_grad = jnp.concatenate(
        [rank_grad, fold_map(in_wide_grad), fold_map(out_wide_grad)], axis=1
    ).astype(low_type)
    x_proj_grad = lax.dot_general(
        mixer_low, small_grad, rows_first, preferred_element_type=float_type
    )
    mixer_in_grad = (
        scan_in_grad
        + lax.dot_general(small_grad, x_proj, last_dims, preferred_element_type=float_type)
    )
    inner_x_grad, halo_grad, conv_weight_grad, conv_bias_grad = conv_back(mixer_in_grad)
    edge_grad = shifted_2(halo_grad, "hs", -1)
    edge_total = lax.dynamic_slice_in_dim(inner_x_grad, edge_start, CONV - 1, 0) + edge_grad
    inner_x_grad = lax.dynamic_update_slice_in_dim(inner_x_grad, edge_total, edge_start, 0)
    projected_grad = jnp.concatenate([inner_x_grad.astype(low_type), gate_pre_low], axis=1)
    in_proj_grad = lax.dot_general(
        normed_low, projected_grad, rows_first, preferred_element_type=float_type
    )
    normed_one_grad = lax.dot_general(
        projected_grad, in_proj, last_dims, preferred_element_type=float_type
    )
    tokens_norm_grad, gain_mix_grad = norm_one_back(normed_one_grad)
    tokens_grad = middle_grad + tokens_norm_grad
    gains_local = jnp.concatenate([gain_mix_grad, gain_ffn_grad])
    columns = [
        x_proj_grad,
        dt_proj_grad,
        log_grad.T,
        conv_weight_grad.T,
        conv_bias_grad[:, None],
        dt_bias_grad[:, None],
        skip_grad.T,
        gains_local[:, None],
        router_grad.reshape(inner_width, -1),
    ]
    packed = jnp.concatenate(columns, axis=1)
    summed = lax.psum_scatter(packed, ("ep", "hs"), scatter_dimension=0, tiled=True)
    pieces, at = [], 0
    for column in columns:
        pieces.append(summed[:, at : at + column.shape[1]])
        at += column.shape[1]
    x_proj_sum = pieces[0]
    dt_proj_sum = pieces[1].T
    a_log_sum = pieces[2]
    conv_weight_sum = pieces[3].T
    conv_bias_sum, dt_bias_sum, skip_sum, gains_sum = [p[:, 0] for p in pieces[4:8]]
    router_sum = pieces[8].reshape(-1)
    in_proj_sum = lax.psum_scatter(
        in_proj_grad.astype(low_type), ("ep", "hs"), scatter_dimension=1, tiled=True
    ).astype(float_type)
    out_proj_sum = lax.psum_scatter(
        out_proj_grad.astype(low_type), ("ep", "hs"), scatter_dimension=0, tiled=True
    ).astype(float_type)
    return (
        block_out,
        tokens_grad,
        gains_sum,
        router_sum,
        in_proj_sum,
        conv_weight_sum,
        conv_bias_sum,
        x_proj_sum,
        dt_proj_sum,
        dt_bias_sum,
        a_log_sum,
        skip_sum,
        out_proj_sum,
        up_grad[None],
        down_grad[None],
    )


def solution(mesh):
    return jax.shard_map(
        body,
        mesh=mesh,
        in_specs=(
            P(("ep", "hs"), None),
            P(("ep", "hs")),
            P(("ep", "hs")),
            P(("ep", "hs")),
            P(("ep", "hs")),
            P(),
            P(),
            P(),
            P(),
            P(),
            P(),
            P(),
            P(),
            P(),
            P(),
            P(),
            P(),
            P("ep", None, "hs"),
            P("ep", "hs", None),
            P(("ep", "hs"), None),
        ),
        out_specs=(
            P(("ep", "hs"), None),
            P(("ep", "hs"), None),
            P(("ep", "hs")),
            P(("ep", "hs")),
            P(None, ("ep", "hs")),
            P(None, ("ep", "hs")),
            P(("ep", "hs")),
            P(("ep", "hs"), None),
            P(None, ("ep", "hs")),
            P(("ep", "hs")),
            P(("ep", "hs"), None),
            P(("ep", "hs")),
            P(("ep", "hs"), None),
            P("ep", None, "hs"),
            P("ep", "hs", None),
        ),
        check_vma=False,
    )
```

time: 2310 us -> 1030 us (0.45)
  local copies, waits for them, and re-layouts: 644 us -> 49.4 us
  other arithmetic: 481 us -> 36.4 us
  waiting for transfers between devices: 919 us -> 555 us
  Pallas kernels: 0 us -> 166 us
    unnamed x13 -> x9, waiting for transfers between devices: 461 us -> 170 us
    squeeze x192 -> x0, local copies, waits for them, and re-layouts: 228 us -> none  [the longest x160 170 us: block_summaries(): block_ends, _ = lax.scan(jax.checkpoint(advance), initial, sequence)]
    reduce_sum x50 -> x2, other arithmetic: 207 us -> 5.93 us  [fold_map(): summed = jnp.sum(wide, axis=3)]
    pallas_call x0 -> x4, Pallas kernels: none -> 166 us  [the longest x1 75.7 us: scan_grads(): pl.pallas_call(grads_kernel, grid=(width // LANES,), in_specs=[tile(rows)...]
    dynamic_update_slice x112 -> x0, local copies, waits for them, and re-layouts: 115 us -> none  [the longest x96 62.7 us: block_outputs(): _, readout = lax.scan(jax.checkpoint(advance), opening, sequence)]
    pad x31 -> x0, local copies, waits for them, and re-layouts: 107 us -> none  [block_summaries(): return lax.associative_scan(join_forward, (block_spans, block_ends), axis=0)]
    add x33 -> x0, other arithmetic: 85.2 us -> none  [the longest x16 57.8 us: advance(): return (decays * memory + driven[:, :, None] * in_map[:, None, :], None)]
    reduce_scatter x1, waiting for transfers between devices: 227 us -> 145 us  [body(): lax.psum_scatter(in_proj_grad.astype(low_type), ('ep', 'hs'), scatter_dim...]
  transfers between devices with their start and end apart: 14 -> 12, of which waited for: 9 -> 8; matrix products, arithmetic and copies ran while one was open for 4% -> 9% of each run, Pallas kernels for 0% -> 0%
where the time goes in v1:
time: 1030 us; the launch traced here: 1020 us
  waiting for transfers between devices  555 us (54%)
  Pallas kernels  166 us (16%)
  matrix products  101 us (10%)
  blocking collectives  72 us (7%)
  local copies, waits for them, and re-layouts  49.4 us (5%)
  other arithmetic  36.4 us (4%)
  starting transfers between devices  19.1 us (2%)
  between operations  16.6 us (2%)
    unnamed x9, waiting for transfers between devices  170 us
    reduce_scatter x1, waiting for transfers between devices, body(): lax.psum_scatter(in_proj_grad.astype(low_type), ('ep', 'hs'), scatter_dim...  145 us
    reduce_scatter x1, waiting for transfers between devices, body(): lax.psum_scatter(partial_out, 'hs', scatter_dimension=0, tiled=True)  91.8 us
    pallas_call x1, Pallas kernels, scan_grads(): pl.pallas_call(grads_kernel, grid=(width // LANES,), in_specs=[tile(rows)...  75.7 us
    reduce_scatter x1, waiting for transfers between devices, body(): lax.psum_scatter(partial_grad.astype(jnp.bfloat16), 'hs', scatter_dimensi...  54.5 us
    all_gather x1, waiting for transfers between devices, body(): lax.all_gather(arrived_grad, 'hs', axis=0, tiled=True)  48.3 us
    pallas_call x1, Pallas kernels, scan_outputs(): pl.pallas_call(outputs_kernel, grid=(width // LANES,), in_specs=[tile(row...  37.4 us
    all_gather x1, waiting for transfers between devices, body(): lax.all_gather(arrived, 'hs', axis=0, tiled=True).reshape(-1, model_width)  36 us
  transfers between devices with their start and end apart: 12, of which 8 were waited for; matrix products, arithmetic and copies ran while one was open for 9% of the time, Pallas kernels for 0%

profile of v1, /device:TPU:0, one launch (start us, length us, event | category | flops | bytes accessed | tf_op | source)
XLA Modules:
  0.0 1015.2 jit_solution(7451224214762169512)
XLA Ops:
  8.8 4.9 collective-permute-start.1
  15.5 6.3 fusion.68
  34.0 7.4 fusion.16
  48.7 24.9 %scan_ends.1 = (f32[128,2304]{1,0:T(8,128)}, f32[8,2304]{1,0:T(8,128)}, f32[16,2304]{1,0:T(8,128)}, f32[1,2304]{1,0:T(1,128)}) custom-call(f32[256,2304]{1,0:T(8,128)} %copy-done.2, f32[256,2304]{1,0:T(8,128)} %get-tuple-element.133.dt, f32[256,16]{1,0:T(8,128)} %copy.63.in_map, f32[256,1]{1,0:T(8,128)} %copy.51.starts, f32[16,2304]{1,0:T(8,128)} %negate_bitcast_fusion.rates), custom_call_target="tpu_custom_call" | custom-call | tf_op jit(solution)/shard_map/scan_ends/pallas_call | solution.py:270
  73.6 13.3 %all-gather.3 = f32[4,1,2304]{2,1,0:T(1,128)S(1)} all-gather(f32[1,1,2304]{2,1,0:T(1,128)} %bitcast.89), channel_id=2, replica_groups=mesh['ep'=8,'hs'=4] {'hs'}, dimensions={0}, use_global_device_ids=true | all-gather | bytes 46080 | tf_op jit(solution)/shard_map/all_gather | solution.py:359
  88.5 13.9 %all-gather.1 = bf16[64,2304]{1,0:T(8,128)(2,1)S(1)} all-gather(bf16[16,2304]{1,0:T(8,128)(2,1)S(1)} %convert_element_type.94), channel_id=3, replica_groups=mesh['ep'=8,'hs'=4] {'hs'}, dimensions={0}, use_global_device_ids=true | all-gather | bytes 368640 | tf_op jit(solution)/shard_map/all_gather | solution.py:360
  103.2 37.4 %scan_outputs.1 = (f32[256,2304]{1,0:T(8,128)}, bf16[256,2304]{1,0:T(8,128)(2,1)}) custom-call(f32[256,2304]{1,0:T(8,128)} %copy-done.2, f32[256,2304]{1,0:T(8,128)} %get-tuple-element.133.dt, f32[256,16]{1,0:T(8,128)} %copy.63.in_map, f32[256,16]{1,0:T(8,128)} %copy.64.out_map, f32[256,1]{1,0:T(8,128)} %copy.51.starts, ...), custom_call_target="tpu_custom_call" | custom-call | tf_op jit(solution)/shard_map/scan_outputs/pallas_call | solution.py:286
  140.7 4.7 multiply_reduce_fusion.6
  146.5 15.7 %all_to_all.20 = bf16[8,40,1152]{2,1,0:T(8,128)(2,1)} all-to-all(bf16[8,40,1152]{2,1,0:T(8,128)(2,1)S(1)} %bitcast.79), channel_id=1, replica_groups=mesh['ep'=8,'hs'=4] {'ep'}, dimensions={0} | all-to-all | bytes 1474560 | tf_op jit(solution)/shard_map/all_to_all | solution.py:502
  168.8 15.1 %all_to_all.21 = bf16[8,40,1152]{2,1,0:T(8,128)(2,1)} all-to-all(bf16[8,40,1152]{2,1,0:T(8,128)(2,1)S(1)} %bitcast.80), channel_id=1, replica_groups=mesh['ep'=8,'hs'=4] {'ep'}, dimensions={0} | all-to-all | bytes 1474560 | tf_op jit(solution)/shard_map/all_to_all | solution.py:531
  184.1 36.0 %all-gather.7.cloned.1.call-done = bf16[32,40,1152]{2,1,0:T(8,128)(2,1)} async-done(((bf16[8,40,1152]{2,1,0:T(8,128)(2,1)}), bf16[32,40,1152]{2,1,0:T(8,128)(2,1)}) %all-gather.7.cloned.1.call-update) | async-done | bytes 2949136 | tf_op jit(solution)/shard_map/all_gather | solution.py:509
  220.1 5.1 fusion.24
  227.0 5.2 fusion.19
  232.3 48.3 %all-gather.9.cloned.1.call-done = bf16[32,40,1152]{2,1,0:T(8,128)(2,1)} async-done(((bf16[8,40,1152]{2,1,0:T(8,128)(2,1)}), bf16[32,40,1152]{2,1,0:T(8,128)(2,1)}) %all-gather.9.cloned.1.call-update) | async-done | bytes 2949136 | tf_op jit(solution)/shard_map/all_gather | solution.py:538
  280.6 8.2 fusion.6
  294.2 91.8 %reduce-scatter.10.cloned.1.call-done = f32[320,1152]{1,0:T(8,128)} async-done(((f32[1280,1152]{1,0:T(8,128)}), f32[320,1152]{1,0:T(8,128)}) %reduce-scatter.10.cloned.1.call-update) | async-done | bytes 1474576 | tf_op jit(solution)/shard_map/reduce_scatter | solution.py:514
  392.0 54.5 %reduce-scatter.12.cloned.1.call-done = bf16[320,1152]{1,0:T(8,128)(2,1)} async-done(((bf16[1280,1152]{1,0:T(8,128)(2,1)}), bf16[320,1152]{1,0:T(8,128)(2,1)}) %reduce-scatter.12.cloned.1.call-update) | async-done | bytes 737296 | tf_op jit(solution)/shard_map/reduce_scatter | solution.py:553
  453.9 9.1 all-to-all-done.3
  466.8 6.1 fusion.93.gated_grad
  472.9 27.5 %scan_adjoints.1 = (f32[256,2304]{1,0:T(8,128)}, bf16[256,2304]{1,0:T(8,128)(2,1)}, f32[128,2304]{1,0:T(8,128)}, f32[8,2304]{1,0:T(8,128)}, f32[16,2304]{1,0:T(8,128)}) custom-call(f32[256,2304]{1,0:T(8,128)} %fusion.93.gated_grad, f32[256,2304]{1,0:T(8,128)} %get-tuple-element.117.gate, f32[256,2304]{1,0:T(8,128)} %get-tuple-element.37.scan_out, ...), custom_call_target="tpu_custom_call" | custom-call | tf_op jit(solution)/shard_map/scan_adjoints/pallas_call | solution.py:302
  501.4 13.9 %all-gather.2 = bf16[64,2304]{1,0:T(8,128)(2,1)S(1)} all-gather(bf16[16,2304]{1,0:T(8,128)(2,1)S(1)} %convert_element_type.107), channel_id=4, replica_groups=mesh['ep'=8,'hs'=4] {'hs'}, dimensions={0}, use_global_device_ids=true | all-gather | bytes 368640 | tf_op jit(solution)/shard_map/all_gather | solution.py:369
  516.1 75.7 %scan_grads.1 = (f32[256,2304]{1,0:T(8,128)}, f32[256,2304]{1,0:T(8,128)}, f32[32,16,8,128]{3,2,1,0:T(8,128)}, f32[32,16,8,128]{3,2,1,0:T(8,128)}, f32[16,2304]{1,0:T(8,128)}, /*index=5*/f32[1,2304]{1,0:T(1,128)}) custom-call(f32[256,2304]{1,0:T(8,128)} %copy-done.2, f32[256,2304]{1,0:T(8,128)} %get-tuple-element.133.dt, f32[256,16]{1,0:T(8,128)} %copy.63.in_map, ...), custom_call_target="tpu_custom_call" | custom-call | tf_op jit(solution)/shard_map/scan_grads/pallas_call | solution.py:322
  591.9 4.4 fusion.94
  613.1 7.6 multiply_reduce_fusion.3
  634.8 8.4 fusion.30
  643.3 5.1 concatenate.24
  657.1 8.6 convolution_convert_fusion
  665.8 7.0 convolution_bitcast_fusion.1
  672.8 4.9 convolution_bitcast_fusion
  679.1 71.3 %reduce-scatter.16.cloned.1.call-done = f32[72,204]{1,0:T(8,128)} async-done(((f32[2304,204]{1,0:T(8,128)}), f32[72,204]{1,0:T(8,128)}) %reduce-scatter.16.cloned.1.call-update) | async-done | bytes 58768
  760.5 98.4 %reduce-scatter.18.cloned.1.call-done = bf16[72,1152]{1,0:T(8,128)(2,1)} async-done(((bf16[2304,1152]{1,0:T(8,128)(2,1)}), bf16[72,1152]{1,0:T(8,128)(2,1)}) %reduce-scatter.18.cloned.1.call-update) | async-done | bytes 165904
  860.6 145.4 %reduce-scatter.14.cloned.1.call-done = bf16[1152,144]{0,1:T(8,128)(2,1)} async-done(((bf16[1152,4608]{0,1:T(8,128)(2,1)}), bf16[1152,144]{0,1:T(8,128)(2,1)}) %reduce-scatter.14.cloned.1.call-update) | async-done | bytes 331792 | tf_op jit(solution)/shard_map/reduce_scatter | solution.py:653
  (314 shorter events, 112.5 us)
Async XLA Ops:
  7.2 219.9 %copy-start = (bf16[1,768,1152]{2,1,0:T(8,128)(2,1)S(1)}, bf16[1,768,1152]{2,1,0:T(8,128)(2,1)}, u32[]{:S(2)}) copy-start(bf16[1,768,1152]{2,1,0:T(8,128)(2,1)} %param.38) | copy-start | bytes 5308420
  7.2 212.9 %all-gather.7.cloned.1.call-start = ((), (), s32[]{:S(2)}) async-start(), calls=%async_computation.9 | async-start | bytes 3686400 | tf_op jit(solution)/shard_map/all_gather | solution.py:509
  8.8 24.5 %collective-permute-start.1 = (f32[3]{0:T(128)S(1)}, f32[3]{0:T(128)S(1)}, u32[]{:S(2)}, u32[]{:S(2)}) collective-permute-start(f32[3]{0:T(128)S(1)} %dynamic_slice.10), channel_id=1, source_target_pairs={{0,1},{1,2},{2,3},{4,5},{5,6},{6,7},{8,9},{9,10},{10,11},{12,13},{... | collective-permute-start | bytes 44 | tf_op jit(solution)/shard_map/ppermute | solution.py:354
  27.4 6.0 collective-permute-start
  31.0 114.4 %copy-start.81 = (pred[256]{0:T(512)(128)(4,1)}, pred[256]{0:T(512)(128)(4,1)S(1)}, u32[]{:S(2)}) copy-start(pred[256]{0:T(512)(128)(4,1)S(1)} %broadcast_compare_fusion) | copy-start | bytes 772
  31.0 114.4 %copy-start.57 = (s32[256]{0:T(256)}, s32[256]{0:T(256)S(1)}, u32[]{:S(2)}) copy-start(s32[256]{0:T(256)S(1)} %multiply_add_fusion.1) | copy-start | bytes 3076
  103.2 37.4 %copy-start.6 = (bf16[256,1152]{1,0:T(8,128)(2,1)S(1)}, bf16[256,1152]{1,0:T(8,128)(2,1)}, u32[]{:S(2)}) copy-start(bf16[256,1152]{1,0:T(8,128)(2,1)} %param.20) | copy-start | bytes 1769476
  103.2 37.4 %copy-start.93 = (f32[256]{0:T(256)S(1)}, f32[256]{0:T(256)}, u32[]{:S(2)}) copy-start(f32[256]{0:T(256)} %copy-done.92) | copy-start | bytes 3076
  145.9 21.1 %copy-start.8 = (bf16[256,1152]{1,0:T(8,128)(2,1)S(1)}, bf16[256,1152]{1,0:T(8,128)(2,1)}, u32[]{:S(2)}) copy-start(bf16[256,1152]{1,0:T(8,128)(2,1)} %param.39) | copy-start | bytes 1769476
  162.2 118.4 %all-gather.9.cloned.1.call-start = ((), (), s32[]{:S(2)}) async-start(), calls=%async_computation.11 | async-start | bytes 3686400 | tf_op jit(solution)/shard_map/all_gather | solution.py:538
  184.0 202.0 %reduce-scatter.10.cloned.1.call-start = ((), (), s32[]{:S(2)}) async-start(), calls=%async_computation.10 | async-start | bytes 7372800 | tf_op jit(solution)/shard_map/reduce_scatter | solution.py:514
  232.3 214.2 %reduce-scatter.12.cloned.1.call-start = ((), (), s32[]{:S(2)}) async-start(), calls=%async_computation.12 | async-start | bytes 3686400 | tf_op jit(solution)/shard_map/reduce_scatter | solution.py:553
  294.2 156.9 %copy-start.58 = (s32[256]{0:T(256)S(1)}, s32[256]{0:T(256)}, u32[]{:S(2)}) copy-start(s32[256]{0:T(256)} %copy-done.57) | copy-start | bytes 3076
  294.2 156.9 %copy-start.82 = (pred[256]{0:T(512)(128)(4,1)S(1)}, pred[256]{0:T(512)(128)(4,1)}, u32[]{:S(2)}) copy-start(pred[256]{0:T(512)(128)(4,1)} %copy-done.81) | copy-start | bytes 772
  388.3 58.2 %all-to-all-start.1 = ((bf16[8,40,1152]{2,1,0:T(8,128)(2,1)}), bf16[8,40,1152]{2,1,0:T(8,128)(2,1)S(1)}, u32[]{:S(2)}, u32[]{:S(2)}) async-start(bf16[8,40,1152]{2,1,0:T(8,128)(2,1)} %bitcast.8), calls=%async_computation.2 | async-start | bytes 1474560 | tf_op jit(solution)/shard_map/all_to_all | solution.py:515
  392.0 60.7 %copy-start.30 = (f32[1152,8]{0,1:T(8,128)S(1)}, f32[1152,8]{0,1:T(8,128)}, u32[]{:S(2)}) copy-start(f32[1152,8]{0,1:T(8,128)} %param.36) | copy-start | bytes 110596
  392.0 60.7 %copy-start.62 = (f32[256]{0:T(256)S(1)}, f32[256]{0:T(256)}, u32[]{:S(2)}) copy-start(f32[256]{0:T(256)} %copy-done.61) | copy-start | bytes 3076
  392.0 60.7 %copy-start.65 = (f32[256]{0:T(256)S(1)}, f32[256]{0:T(256)}, u32[]{:S(2)}) copy-start(f32[256]{0:T(256)} %copy-done.64) | copy-start | bytes 3076
  392.0 60.7 %copy-start.68 = (s32[256]{0:T(256)S(1)}, s32[256]{0:T(256)}, u32[]{:S(2)}) copy-start(s32[256]{0:T(256)} %param.23) | copy-start | bytes 3076
  392.0 60.7 %copy-start.71 = (f32[256]{0:T(256)S(1)}, f32[256]{0:T(256)}, u32[]{:S(2)}) copy-start(f32[256]{0:T(256)} %copy-done.70) | copy-start | bytes 3076
  446.5 16.4 %copy-start.49 = (f32[256]{0:T(256)S(1)}, f32[256]{0:T(256)}, u32[]{:S(2)}) copy-start(f32[256]{0:T(256)} %copy-done.48) | copy-start | bytes 3076
  446.5 16.4 %all-to-all-start.3 = ((bf16[8,40,1152]{2,1,0:T(8,128)(2,1)}), bf16[8,40,1152]{2,1,0:T(8,128)(2,1)}, u32[]{:S(2)}, u32[]{:S(2)}) async-start(bf16[8,40,1152]{2,1,0:T(8,128)(2,1)} %bitcast.82), calls=%async_computation.5 | async-start | bytes 1474560 | tf_op jit(solution)/shard_map/all_to_all | solution.py:557
  450.9 299.5 %reduce-scatter.16.cloned.1.call-start = ((), (), s32[]{:S(2)}) async-start(), calls=%async_computation.14 | async-start | bytes 2433024
  472.9 42.4 %copy-start.19 = (f32[2304,16]{0,1:T(8,128)S(1)}, f32[2304,16]{0,1:T(8,128)}, u32[]{:S(2)}) copy-start(f32[2304,16]{0,1:T(8,128)} %param.32) | copy-start | bytes 442372
  472.9 42.4 %copy-start.35 = (f32[2304]{0:T(1024)S(1)}, f32[2304]{0:T(1024)}, u32[]{:S(2)}) copy-start(f32[2304]{0:T(1024)} %copy-done.34) | copy-start | bytes 27652
  472.9 42.5 %copy-start.37 = (f32[2304]{0:T(1024)S(1)}, f32[2304]{0:T(1024)}, u32[]{:S(2)}) copy-start(f32[2304]{0:T(1024)} %copy-done.36) | copy-start | bytes 27652
  472.9 42.5 %copy-start.46 = (f32[2304]{0:T(1024)S(1)}, f32[2304]{0:T(1024)}, u32[]{:S(2)}) copy-start(f32[2304]{0:T(1024)} %get-tuple-element.103) | copy-start | bytes 27652
  516.1 75.7 %copy-start.16 = (f32[256,2304]{1,0:T(8,128)S(1)}, f32[256,2304]{1,0:T(8,128)}, u32[]{:S(2)}) copy-start(f32[256,2304]{1,0:T(8,128)} %get-tuple-element.134) | copy-start | bytes 7077892
  621.9 9.8 collective-permute-start.2
  651.6 207.3 %reduce-scatter.18.cloned.1.call-start = ((), (), s32[]{:S(2)}) async-start(), calls=%async_computation.15 | async-start | bytes 5474304
  655.9 350.2 %reduce-scatter.14.cloned.1.call-start = ((), (), s32[]{:S(2)}) async-start(), calls=%async_computation.13 | async-start | bytes 10948608 | tf_op jit(solution)/shard_map/reduce_scatter | solution.py:653
  677.7 330.2 %copy-start.1 = (bf16[1,768,1152]{2,1,0:T(8,128)(2,1)S(1)}, bf16[1,768,1152]{2,1,0:T(8,128)(2,1)}, u32[]{:S(2)}) copy-start(bf16[1,768,1152]{2,1,0:T(8,128)(2,1)} %param.38) | copy-start | bytes 5308420
  (83 other events, 411.6 us)
Sparse Core Ops, SparseCore 0:
  162.3 57.6 all-gather.6
  221.6 58.9 all-gather.8
  282.9 103.0 reduce-scatter.9
  388.7 57.7 reduce-scatter.11
  651.7 98.5 reduce-scatter.15
  755.9 103.0 reduce-scatter.17
  865.0 140.9 reduce-scatter.13

commit v2 on v0

v2 whole, which is shorter than its diff:
```python
import jax
import jax.numpy as jnp
from jax import lax
from jax.experimental import pallas as pl
from jax.experimental.pallas import tpu as pltpu
from jax.sharding import PartitionSpec as P

DT_RANK = 72
CONV = 4
STATE = 16
SEGMENTS = 8
LANES = 128
TILES = 3
RESET = 1e30
LN2 = 0.6931471805599453


def widened(values):
    shaped = values.reshape(SEGMENTS, -1, values.shape[1])
    shaped = jnp.transpose(shaped, (1, 2, 0))[..., None]
    return jnp.broadcast_to(shaped, shaped.shape[:3] + (LANES,))


def each_tile(work):
    @pl.loop(0, TILES)
    def _(k):
        work(pl.ds(pl.multiple_of(k * LANES, LANES), LANES))


def spread_rates(target, rates, lanes):
    for n in range(STATE):
        target[n] = jnp.broadcast_to(rates[n : n + 1, lanes], (SEGMENTS, LANES))


def ends_kernel(x, dt, in_wide, big, rates, ends_ex, cum_ex, end_all, cum_all,
                rate_wide, end_scr, sum_scr, x_scr, dt_scr):
    steps = x.shape[0] // SEGMENTS

    def work(lanes):
        spread_rates(rate_wide, rates, lanes)
        x_scr[...] = x[:, lanes]
        dt_scr[...] = dt[:, lanes]

        def step(i, carry):
            total, states = carry[0], carry[1:]
            rows = pl.ds(i, SEGMENTS, stride=steps)
            stride = dt_scr[rows, :]
            driven = stride * x_scr[rows, :]
            stride = stride + big[i, 0]
            new = [total + stride]
            for n in range(STATE):
                new.append(jnp.exp2(stride * rate_wide[n]) * states[n] + driven * in_wide[i, n])
            return tuple(new)

        zero = jnp.zeros((SEGMENTS, LANES), jnp.float32)
        done = lax.fori_loop(0, steps, step, (zero,) * (STATE + 1), unroll=4)
        sum_scr[...] = done[0]
        for n in range(STATE):
            end_scr[n * SEGMENTS : (n + 1) * SEGMENTS, :] = done[1 + n]
        state = jnp.zeros((STATE, LANES), jnp.float32)
        cum = jnp.zeros((1, LANES), jnp.float32)
        for s in range(SEGMENTS):
            ends_ex[s * STATE : (s + 1) * STATE, lanes] = state
            cum_ex[s : s + 1, lanes] = cum
            own = sum_scr[s : s + 1, :]
            state = (
                jnp.exp2(own * rates[:, lanes]) * state
                + end_scr[pl.ds(s, STATE, stride=SEGMENTS), :]
            )
            cum = cum + own
        end_all[:, lanes] = state
        cum_all[:, lanes] = cum

    each_tile(work)


def opening_states(cum, rate_wide, entering, ends_ex, end_scr, lanes):
    end_scr[...] = ends_ex[:, lanes]
    return tuple(
        jnp.exp2(cum * rate_wide[n]) * entering[n : n + 1, lanes]
        + end_scr[pl.ds(n, SEGMENTS, stride=STATE), :]
        for n in range(STATE)
    )


def outputs_kernel(x, dt, in_wide, out_wide, big, rates, ends_ex, cum_ex, entering, skip, gate,
                   scan_out, gated, rate_wide, end_scr, x_scr, dt_scr, out_scr):
    steps = x.shape[0] // SEGMENTS

    def work(lanes):
        spread_rates(rate_wide, rates, lanes)
        x_scr[...] = x[:, lanes]
        dt_scr[...] = dt[:, lanes]
        opening = opening_states(cum_ex[:, lanes], rate_wide, entering, ends_ex, end_scr, lanes)

        def step(i, states):
            rows = pl.ds(i, SEGMENTS, stride=steps)
            stride = dt_scr[rows, :]
            driven = stride * x_scr[rows, :]
            stride = stride + big[i, 0]
            new, total = [], None
            for n in range(STATE):
                state = jnp.exp2(stride * rate_wide[n]) * states[n] + driven * in_wide[i, n]
                new.append(state)
                term = state * out_wide[i, n]
                total = term if total is None else total + term
            out_scr[rows, :] = total
            return tuple(new)

        lax.fori_loop(0, steps, step, opening, unroll=4)
        value = out_scr[...] + skip[:, lanes] * x_scr[...]
        scan_out[:, lanes] = value
        gated[:, lanes] = (value * jax.nn.silu(gate[:, lanes])).astype(gated.dtype)

    each_tile(work)


def adjoint_kernel(gated_grad, gate, scan_out, dt, out_wide, big, rates,
                   scan_grad, gate_grad, adj_ex, cum_ex, adj_all,
                   rate_wide, end_scr, sum_scr, grad_scr, dt_scr):
    steps = dt.shape[0] // SEGMENTS

    def work(lanes):
        spread_rates(rate_wide, rates, lanes)
        incoming = gated_grad[:, lanes]
        gate_in = gate[:, lanes]
        chance = jax.nn.sigmoid(gate_in)
        moved = incoming * (gate_in * chance)
        scan_grad[:, lanes] = moved
        grad_scr[...] = moved
        dt_scr[...] = dt[:, lanes]
        gate_grad[:, lanes] = (
            incoming * scan_out[:, lanes] * (chance * (1.0 + gate_in * (1.0 - chance)))
        ).astype(gate_grad.dtype)

        def step(k, carry):
            i = steps - 1 - k
            total, tails = carry[0], carry[1:]
            rows = pl.ds(i, SEGMENTS, stride=steps)
            grad = grad_scr[rows, :]
            stride = dt_scr[rows, :] + big[i, 0]
            new = [total + stride]
            for n in range(STATE):
                new.append(jnp.exp2(stride * rate_wide[n]) * (grad * out_wide[i, n] + tails[n]))
            return tuple(new)

        zero = jnp.zeros((SEGMENTS, LANES), jnp.float32)
        done = lax.fori_loop(0, steps, step, (zero,) * (STATE + 1), unroll=4)
        sum_scr[...] = done[0]
        for n in range(STATE):
            end_scr[n * SEGMENTS : (n + 1) * SEGMENTS, :] = done[1 + n]
        tail = jnp.zeros((STATE, LANES), jnp.float32)
        cum = jnp.zeros((1, LANES), jnp.float32)
        for s in reversed(range(SEGMENTS)):
            adj_ex[s * STATE : (s + 1) * STATE, lanes] = tail
            cum_ex[s : s + 1, lanes] = cum
            own = sum_scr[s : s + 1, :]
            tail = (
                jnp.exp2(own * rates[:, lanes]) * tail
                + end_scr[pl.ds(s, STATE, stride=SEGMENTS), :]
            )
            cum = cum + own
        adj_all[:, lanes] = tail

    each_tile(work)


def grads_kernel(x, dt, in_wide, out_wide, big, rates, ends_ex, cum_ex, entering, skip,
                 scan_grad, adj_ex, back_cum_ex, returning,
                 x_grad, dt_grad, map_grad, log_grad, skip_grad,
                 rate_wide, kept, log_scr, end_scr, x_scr, dt_scr, grad_scr, x_out, dt_out):
    steps = x.shape[0] // SEGMENTS

    @pl.when(pl.program_id(0) == 0)
    def _():
        map_grad[...] = jnp.zeros_like(map_grad)

    def work(lanes):
        spread_rates(rate_wide, rates, lanes)
        x_scr[...] = x[:, lanes]
        dt_scr[...] = dt[:, lanes]
        opening = opening_states(cum_ex[:, lanes], rate_wide, entering, ends_ex, end_scr, lanes)

        def forward(i, states):
            rows = pl.ds(i, SEGMENTS, stride=steps)
            stride = dt_scr[rows, :]
            driven = stride * x_scr[rows, :]
            stride = stride + big[i, 0]
            new = []
            for n in range(STATE):
                remain = jnp.exp2(stride * rate_wide[n]) * states[n]
                kept[i, n] = remain
                new.append(remain + driven * in_wide[i, n])
            return tuple(new)

        lax.fori_loop(0, steps, forward, opening, unroll=4)
        tails = opening_states(back_cum_ex[:, lanes], rate_wide, returning, adj_ex, end_scr, lanes)
        zero = jnp.zeros((SEGMENTS, LANES), jnp.float32)
        for n in range(STATE):
            log_scr[n] = zero

        def backward(k, tails):
            i = steps - 1 - k
            rows = pl.ds(i, SEGMENTS, stride=steps)
            stride = dt_scr[rows, :]
            value = x_scr[rows, :]
            driven = stride * value
            grad = grad_scr[rows, :]
            marked = stride + big[i, 0]
            new = []
            drive_sum, rate_sum = None, None
            for n in range(STATE):
                rate = rate_wide[n]
                in_n = in_wide[i, n]
                adjoint = grad * out_wide[i, n] + tails[n]
                remain = kept[i, n]
                map_grad[1, i, n] += grad * (remain + driven * in_n)
                map_grad[0, i, n] += adjoint * driven
                drive = adjoint * in_n
                touched = adjoint * remain
                slope = touched * rate
                log_scr[n] += touched * stride
                drive_sum = drive if drive_sum is None else drive_sum + drive
                rate_sum = slope if rate_sum is None else rate_sum + slope
                new.append(jnp.exp2(marked * rate) * adjoint)
            x_out[rows, :] = stride * drive_sum
            dt_out[rows, :] = value * drive_sum + LN2 * rate_sum
            return tuple(new)

        grad_scr[...] = scan_grad[:, lanes]
        lax.fori_loop(0, steps, backward, tails, unroll=2)
        dt_grad[:, lanes] = dt_out[...]
        x_grad[:, lanes] = x_out[...] + skip[:, lanes] * grad_scr[...]
        skip_grad[:, lanes] = jnp.sum(grad_scr[...] * x_scr[...], axis=0, keepdims=True)
        for n in range(STATE):
            log_grad[n : n + 1, lanes] = (
                jnp.sum(log_scr[n], axis=0, keepdims=True) * rates[n : n + 1, lanes] * LN2
            )

    each_tile(work)


def tile(rows):
    return pl.BlockSpec((rows, TILES * LANES), lambda j: (0, j))


def whole(shape):
    return pl.BlockSpec(shape, lambda j: (0,) * len(shape))


def shape_of(rows, width, dtype=jnp.float32):
    return jax.ShapeDtypeStruct((rows, width), dtype)


PARAMS = pltpu.CompilerParams(
    dimension_semantics=("arbitrary",), vmem_limit_bytes=56 * 1024 * 1024
)
RATE = pltpu.VMEM((STATE, SEGMENTS, LANES), jnp.float32)
ENDS = pltpu.VMEM((SEGMENTS * STATE, LANES), jnp.float32)
SUMS = pltpu.VMEM((SEGMENTS, LANES), jnp.float32)


def call(kernel, waits, micros, **options):
    specs = options.pop("in_specs")

    def waiting(*refs):
        kernel(*refs[: len(specs)], *refs[len(specs) + len(waits) :])

    waiting.__name__ = options["name"]
    run = pl.pallas_call(
        waiting,
        in_specs=specs + [pl.BlockSpec(memory_space=pl.ANY)] * len(waits),
        compiler_params=PARAMS,
        cost_estimate=pl.CostEstimate(
            flops=0, bytes_accessed=micros * 3_000_000, transcendentals=0
        ),
        **options,
    )
    return lambda *operands: run(*operands, *waits)


def rows_of(rows):
    return pltpu.VMEM((rows, LANES), jnp.float32)


def scan_ends(x, dt, in_wide, big, rates, waits=()):
    rows, width = x.shape
    return call(
        ends_kernel,
        waits,
        15,
        grid=(width // (TILES * LANES),),
        in_specs=[tile(rows), tile(rows), whole(in_wide.shape), whole(big.shape), tile(STATE)],
        out_specs=[tile(SEGMENTS * STATE), tile(SEGMENTS), tile(STATE), tile(1)],
        out_shape=[shape_of(SEGMENTS * STATE, width), shape_of(SEGMENTS, width),
                   shape_of(STATE, width), shape_of(1, width)],
        scratch_shapes=[RATE, ENDS, SUMS, rows_of(rows), rows_of(rows)],
        name="scan_ends",
    )(x, dt, in_wide, big, rates)


def scan_outputs(x, dt, in_wide, out_wide, big, rates, ends_ex, cum_ex, entering, skip, gate, waits=()):
    rows, width = x.shape
    return call(
        outputs_kernel,
        waits,
        20,
        grid=(width // (TILES * LANES),),
        in_specs=[tile(rows), tile(rows), whole(in_wide.shape), whole(out_wide.shape),
                  whole(big.shape), tile(STATE), tile(SEGMENTS * STATE), tile(SEGMENTS),
                  tile(STATE), tile(1), tile(rows)],
        out_specs=[tile(rows), tile(rows)],
        out_shape=[shape_of(rows, width), shape_of(rows, width, jnp.bfloat16)],
        scratch_shapes=[RATE, ENDS] + [rows_of(rows)] * 3,
        name="scan_outputs",
    )(x, dt, in_wide, out_wide, big, rates, ends_ex, cum_ex, entering, skip, gate)


def scan_adjoints(gated_grad, gate, scan_out, dt, out_wide, big, rates, waits=()):
    rows, width = dt.shape
    return call(
        adjoint_kernel,
        waits,
        17,
        grid=(width // (TILES * LANES),),
        in_specs=[tile(rows), tile(rows), tile(rows), tile(rows), whole(out_wide.shape),
                  whole(big.shape), tile(STATE)],
        out_specs=[tile(rows), tile(rows), tile(SEGMENTS * STATE), tile(SEGMENTS), tile(STATE)],
        out_shape=[shape_of(rows, width), shape_of(rows, width, jnp.bfloat16),
                   shape_of(SEGMENTS * STATE, width), shape_of(SEGMENTS, width),
                   shape_of(STATE, width)],
        scratch_shapes=[RATE, ENDS, SUMS, rows_of(rows), rows_of(rows)],
        name="scan_adjoints",
    )(gated_grad, gate, scan_out, dt, out_wide, big, rates)


def scan_grads(x, dt, in_wide, out_wide, big, rates, ends_ex, cum_ex, entering, skip,
               scan_grad, adj_ex, back_cum_ex, returning, waits=()):
    rows, width = x.shape
    steps = rows // SEGMENTS
    wide_shape = (steps, STATE, SEGMENTS, LANES)
    return call(
        grads_kernel,
        waits,
        55,
        grid=(width // (TILES * LANES),),
        in_specs=[tile(rows), tile(rows), whole(in_wide.shape), whole(out_wide.shape),
                  whole(big.shape), tile(STATE), tile(SEGMENTS * STATE), tile(SEGMENTS),
                  tile(STATE), tile(1), tile(rows), tile(SEGMENTS * STATE), tile(SEGMENTS),
                  tile(STATE)],
        out_specs=[tile(rows), tile(rows), whole((2,) + wide_shape), tile(STATE), tile(1)],
        out_shape=[shape_of(rows, width), shape_of(rows, width),
                   jax.ShapeDtypeStruct((2,) + wide_shape, jnp.float32),
                   shape_of(STATE, width), shape_of(1, width)],
        scratch_shapes=[RATE, pltpu.VMEM(wide_shape, jnp.float32), RATE, ENDS]
        + [rows_of(rows)] * 5,
        name="scan_grads",
    )(x, dt, in_wide, out_wide, big, rates, ends_ex, cum_ex, entering, skip, scan_grad, adj_ex,
      back_cum_ex, returning)


def fold_maps(wide):
    summed = jnp.sum(wide, axis=4)
    return jnp.transpose(summed, (3, 1, 0, 2)).reshape(-1, 2 * STATE)


norm_epsilon = 1e-05
highest = lax.Precision.HIGHEST
ROWS_FIRST = (((0,), (0,)), ((), ()))
LAST_DIMS = (((1,), (1,)), ((), ()))


def shifted_2(block, axis, distance):
    devices = range(lax.axis_size(axis))
    route = [(i - distance, i) for i in devices if i - distance in devices]
    return lax.ppermute(block, axis, route)


def crossed(block, axis, mask):
    return lax.ppermute(block, axis, [(i, i ^ mask) for i in range(lax.axis_size(axis))])


def exchanged(blocks, axis):
    return [block if k == 0 else crossed(block, axis, k) for k, block in enumerate(blocks)]


def after(value, *others):
    return lax.optimization_barrier((value,) + others)[0]


def summed_shares(parts, axis):
    count, mine = lax.axis_size(axis), lax.axis_index(axis)
    total = lax.dynamic_index_in_dim(parts, mine, 0, False)
    for shift in range(1, count):
        share = lax.dynamic_index_in_dim(parts, lax.rem(mine + shift, count), 0, False)
        route = [(i, (i + shift) % count) for i in range(count)]
        total = total + lax.ppermute(share.astype(jnp.bfloat16), axis, route).astype(jnp.float32)
    return total


def state_before(cum, end, rates, axis):
    count, mine = lax.axis_size(axis), lax.axis_index(axis)
    first = lax.reduce_precision(cum, 8, 7)
    second = lax.reduce_precision(cum - first, 8, 7)
    sent = jnp.concatenate([end, first, second, cum - first - second], axis=0)
    got = lax.all_gather(sent.astype(jnp.bfloat16), axis).astype(jnp.float32)
    ends, terms = got[:, : end.shape[0]], got[:, end.shape[0] :]
    cums = jnp.sum(terms, axis=1, keepdims=True)
    state = jnp.zeros_like(end)
    for d in range(count - 1):
        state = jnp.where(d < mine, jnp.exp2(cums[d] * rates) * state + ends[d], state)
    return state, cums


def state_after(cums, tail, rates, axis):
    count, mine = lax.axis_size(axis), lax.axis_index(axis)
    tails = lax.all_gather(tail.astype(jnp.bfloat16), axis).astype(jnp.float32)
    state = jnp.zeros_like(tail)
    for d in reversed(range(1, count)):
        state = jnp.where(d > mine, jnp.exp2(cums[d] * rates) * state + tails[d], state)
    return state


def rms_scale(values):
    return lax.rsqrt(jnp.mean(values * values, axis=1, keepdims=True) + norm_epsilon)


def scaled_norm(values, gain_row):
    return values * rms_scale(values) * gain_row[None, :]


def gelu_tanh(values):
    return jax.nn.gelu(values, approximate=True)


def conv_mix(x_inner, halo_rows, start_flags, conv_w, conv_b):
    tap_count = conv_w.shape[0]
    length = x_inner.shape[0]
    extended = jnp.concatenate([halo_rows, x_inner], axis=0)
    flag_line = jnp.concatenate([jnp.zeros((tap_count - 1,), jnp.float32), start_flags], axis=0)
    result = conv_b[None, :] + conv_w[tap_count - 1][None, :] * x_inner
    survive = jnp.ones((length,), jnp.float32)
    for offset in range(1, tap_count):
        survive = survive * (1.0 - flag_line[tap_count - offset : tap_count - offset + length])
        shifted = extended[tap_count - 1 - offset : tap_count - 1 - offset + length]
        result = result + conv_w[tap_count - 1 - offset][None, :] * shifted * survive[:, None]
    return jax.nn.silu(result)


def delta_apply(step_pre, bias_row, real_rows):
    return jax.nn.softplus(step_pre + bias_row[None, :]) * real_rows[:, None]


def mm(left, right):
    return jnp.dot(left, right, preferred_element_type=jnp.float32)


def mm_t(left, right):
    return lax.dot_general(left, right, LAST_DIMS, preferred_element_type=jnp.float32)


def t_mm(left, right):
    return lax.dot_general(left, right, ROWS_FIRST, preferred_element_type=jnp.float32)


def block_mm(left, right):
    return lax.dot_general(
        left, right, (((0, 2), (0, 1)), ((), ())), preferred_element_type=jnp.float32
    )


def body(
    tokens,
    starts,
    counts,
    routes,
    slot_index,
    gain_mix,
    in_proj,
    conv_weight,
    conv_bias,
    x_proj,
    dt_proj,
    dt_bias,
    a_log,
    skip_gain,
    out_proj,
    gain_ffn,
    router,
    up_proj,
    down_proj,
    out_grad,
):
    float_type = jnp.float32
    low_type = jnp.bfloat16
    length = tokens.shape[0]
    model_width = tokens.shape[1]
    inner_width = conv_bias.shape[0]
    experts = router.shape[1]
    capacity = 5 * length // (4 * experts)
    groups, members = lax.axis_size("ep"), lax.axis_size("hs")
    group, member = lax.axis_index("ep"), lax.axis_index("hs")
    half = groups // 2
    upper = group >= half

    def blocks_home(values):
        return lax.all_to_all(values, "ep", split_axis=0, concat_axis=0, tiled=True)

    def by_owner(values):
        wide = inner_width // (half * members * 2)
        shaped = values.T.reshape(half, members, 2, wide, length)
        return jnp.transpose(shaped, (2, 0, 1, 3, 4)).reshape(groups, -1, length)

    up_own, down_own = up_proj[0], down_proj[0]
    far = members // 2
    masks = range(1, far)
    near = [[first + k for k in range(far)] for first in range(0, members, far)]
    ups = lax.all_gather(up_own, "hs", axis_index_groups=near)
    downs = lax.all_gather(down_own, "hs", axis_index_groups=near)

    edge_start = counts[0] - (CONV - 1)
    start_flags = starts.astype(float_type)
    real_rows = (jnp.arange(length, dtype=jnp.int32) < counts[0]).astype(float_type)
    tokens_float = tokens.astype(float_type)
    normed_one, norm_one_back = jax.vjp(scaled_norm, tokens_float, gain_mix)
    normed_low = normed_one.astype(low_type)
    projected = mm(normed_low, in_proj)
    inner_x = projected[:, :inner_width]
    inner_gate = projected[:, inner_width:]
    edge_rows = lax.dynamic_slice_in_dim(inner_x, edge_start, CONV - 1, 0)
    edge_flags = lax.dynamic_slice_in_dim(start_flags, edge_start, CONV - 1, 0)
    later = [jnp.prod(1.0 - edge_flags[k + 1 :]) for k in range(CONV - 1)]
    edge_mask = jnp.stack(later)[:, None]
    halo_rows = shifted_2(edge_rows * edge_mask, "hs", 1)

    def conv_part(x_part, rows_part, weight_part, bias_part):
        return conv_mix(x_part, rows_part, start_flags, weight_part, bias_part)

    mixer_in, conv_back = jax.vjp(conv_part, inner_x, halo_rows, conv_weight, conv_bias)
    mixer_low = mixer_in.astype(low_type)
    small_proj = mm(mixer_low, x_proj)
    rank_low = small_proj[:, :DT_RANK].astype(low_type)
    step_pre = mm(rank_low, dt_proj)
    input_map = small_proj[:, DT_RANK : DT_RANK + STATE]
    output_map = small_proj[:, DT_RANK + STATE :]

    def step_part(pre_part, bias_part):
        return delta_apply(pre_part, bias_part, real_rows)

    step_size, step_back = jax.vjp(step_part, step_pre, dt_bias)
    in_wide, out_wide = widened(input_map), widened(output_map)
    reset_wide = widened(start_flags[:, None] * RESET)
    rates = -(jnp.exp(a_log) / LN2).T
    skip_row = skip_gain[None, :]
    ends_ex, cum_ex, end_all, cum_all = scan_ends(
        mixer_in, step_size, in_wide, reset_wide, rates
    )
    entering, cums = state_before(cum_all, end_all, rates, "hs")
    scan_out, gated_low = scan_outputs(
        mixer_in,
        step_size,
        in_wide,
        out_wide,
        reset_wide,
        rates,
        ends_ex,
        cum_ex,
        entering,
        skip_row,
        inner_gate,
        waits=[ups],
    )
    mixer_out = mm(gated_low, out_proj)
    middle = tokens_float + mixer_out * real_rows[:, None]
    normed_two, norm_two_back = jax.vjp(scaled_norm, middle, gain_ffn)
    router_probs = jax.nn.softmax(
        jnp.dot(normed_two, router, precision=highest, preferred_element_type=float_type), axis=1
    )
    chosen = (routes[:, None] == jnp.arange(experts, dtype=jnp.int32)[None, :]).astype(float_type)
    gate_value = jnp.sum(router_probs * chosen, axis=1)
    column = routes * capacity + slot_index
    placed = (
        (column[:, None] == jnp.arange(experts * capacity, dtype=jnp.int32)[None, :])
        & (slot_index[:, None] >= 0)
    ).astype(low_type)
    grad_out = out_grad.astype(float_type)
    token_grad = grad_out * gate_value[:, None]

    rows_low = t_mm(placed, normed_two.astype(low_type)).astype(low_type)
    rows_own = blocks_home(rows_low.reshape(experts, capacity, model_width)).reshape(
        -1, model_width
    )
    rows_pair = crossed(rows_own, "hs", far)
    grads_low = t_mm(placed, token_grad.astype(low_type)).astype(low_type)
    grads_own = blocks_home(grads_low.reshape(experts, capacity, model_width)).reshape(
        -1, model_width
    )
    grads_pair = crossed(after(grads_own, rows_pair), "hs", far)
    gated_blocks = blocks_home(after(gated_low, grads_own).T.reshape(groups, -1, length))
    normed_all = lax.all_gather(after(normed_low, grads_own), "ep")
    rows = jnp.concatenate([rows_own, rows_pair], axis=0)
    grads = jnp.concatenate([grads_own, grads_pair], axis=0)
    place = lax.rem(member, far)

    def near_parts(gathered):
        return [
            lax.dynamic_index_in_dim(gathered, jnp.bitwise_xor(place, mask), 0, False)
            for mask in range(far)
        ]

    up_all, down_all = near_parts(ups), near_parts(downs)
    pre_all = [mm(rows, up) for up in up_all]
    hidden_all, gelu_backs = zip(*[jax.vjp(gelu_tanh, pre) for pre in pre_all])
    hidden_all = [hidden.astype(low_type) for hidden in hidden_all]
    expert_part = sum(mm(hidden, down) for hidden, down in zip(hidden_all, down_all))
    count = rows_own.shape[0]

    def pair_sum(partial, *earlier):
        other = crossed(after(partial[count:].astype(low_type), *earlier), "hs", far)
        return (partial[:count] + other.astype(float_type)).astype(low_type)

    home_rows = blocks_home(pair_sum(expert_part, grads_pair).reshape(groups, -1, model_width))
    pre_grads = [
        back(mm_t(grads, down))[0].astype(low_type) for back, down in zip(gelu_backs, down_all)
    ]
    grad_part = sum(mm_t(pre_grad, up) for pre_grad, up in zip(pre_grads, up_all))
    up_parts = [t_mm(rows, pre_grad) for pre_grad in pre_grads]
    down_parts = [t_mm(hidden, grads) for hidden in hidden_all]
    up_sent = [part.astype(low_type) for part in up_parts[1:]]
    down_sent = [part.astype(low_type) for part in down_parts[1:]]
    grad_rows = pair_sum(grad_part)
    grad_rows, up_sent, down_sent = lax.optimization_barrier((grad_rows, up_sent, down_sent))
    home_grad = blocks_home(grad_rows.reshape(groups, -1, model_width))

    expert_out = mm(placed, home_rows.reshape(experts * capacity, model_width))
    block_out = (middle + gate_value[:, None] * expert_out).astype(low_type)
    gate_grad = jnp.sum(grad_out * expert_out, axis=1)
    logit_grad = router_probs * gate_grad[:, None] * (chosen - gate_value[:, None])
    router_grad = lax.dot_general(
        normed_two, logit_grad, ROWS_FIRST, precision=highest, preferred_element_type=float_type
    )
    normed_two_grad = mm(
        placed, home_grad.reshape(experts * capacity, model_width)
    ) + lax.dot_general(
        logit_grad, router, LAST_DIMS, precision=highest, preferred_element_type=float_type
    )
    middle_norm_grad, gain_ffn_grad = norm_two_back(normed_two_grad)
    middle_grad = grad_out + middle_norm_grad
    mixer_grad = (middle_grad * real_rows[:, None]).astype(low_type)
    mixer_grad_all = lax.all_gather(mixer_grad, "ep")
    gated_grad = mm_t(mixer_grad, out_proj)
    scan_grad, gate_pre_low, adj_ex, back_cum_ex, adj_all = scan_adjoints(
        gated_grad,
        inner_gate,
        scan_out,
        step_size,
        out_wide,
        reset_wide,
        rates,
        waits=[gated_blocks],
    )
    returning = state_after(cums, adj_all, rates, "hs")
    returning, up_sent, down_sent, gate_sent = lax.optimization_barrier(
        (returning, up_sent, down_sent, by_owner(gate_pre_low))
    )
    gate_blocks = blocks_home(gate_sent)
    up_got = [crossed(part, "hs", mask) for part, mask in zip(up_sent, masks)]
    scan_in_grad, size_grad, wide_grads, log_grad, skip_grad = scan_grads(
        mixer_in,
        step_size,
        in_wide,
        out_wide,
        reset_wide,
        rates,
        ends_ex,
        cum_ex,
        entering,
        skip_row,
        scan_grad,
        adj_ex,
        back_cum_ex,
        returning,
    )
    size_grad, gate_blocks, up_got, down_sent = lax.optimization_barrier(
        (size_grad, gate_blocks, up_got, down_sent)
    )
    down_got = [crossed(part, "hs", mask) for part, mask in zip(down_sent, masks)]
    pre_step_grad, dt_bias_grad = step_back(size_grad)
    pre_step_low = pre_step_grad.astype(low_type)
    rank_grad = mm_t(pre_step_low, dt_proj)
    small_grad = jnp.concatenate([rank_grad, fold_maps(wide_grads)], axis=1).astype(low_type)
    mixer_in_grad = scan_in_grad + mm_t(small_grad, x_proj)
    inner_x_grad, halo_grad, conv_weight_grad, conv_bias_grad = conv_back(mixer_in_grad)
    edge_grad = shifted_2(halo_grad, "hs", -1) * edge_mask
    edge_total = lax.dynamic_slice_in_dim(inner_x_grad, edge_start, CONV - 1, 0) + edge_grad
    inner_x_grad = lax.dynamic_update_slice_in_dim(inner_x_grad, edge_total, edge_start, 0)
    inner_low = inner_x_grad.astype(low_type)

    inner_sent = by_owner(inner_low)
    inner_blocks = blocks_home(inner_sent)
    gated_blocks = after(gated_blocks, inner_sent)
    gate_blocks = after(gate_blocks, inner_sent)
    small_late, step_late = after(small_grad, inner_sent), after(pre_step_low, inner_sent)

    def row_blocks(values):
        blocks = values.reshape(values.shape[0], groups, -1)
        return blocks_home(jnp.transpose(blocks, (1, 0, 2)))

    def row_shares(blocks):
        part = jnp.sum(blocks.astype(float_type), axis=0)
        shares = part.reshape(part.shape[0], members, -1)
        return summed_shares(jnp.transpose(shares, (1, 0, 2)), "hs")

    pieces = [
        t_mm(small_late, mixer_low),
        t_mm(rank_low, step_late),
        log_grad,
        dt_bias_grad[None, :],
        skip_grad,
        router_grad.reshape(inner_width, -1).T,
    ]
    packed = jnp.concatenate([after(pieces[0], inner_blocks)] + pieces[1:], axis=0)
    packed = row_blocks(packed.astype(low_type))
    inner_low = after(inner_low, inner_blocks)
    normed_one_grad = mm_t(inner_low, in_proj[:, :inner_width]) + mm_t(
        gate_pre_low, in_proj[:, inner_width:]
    )
    tokens_norm_grad, gain_mix_grad = norm_one_back(normed_one_grad)
    tokens_grad = middle_grad + tokens_norm_grad
    late = jnp.concatenate(
        [
            conv_weight_grad,
            conv_bias_grad[None, :],
            jnp.concatenate([gain_mix_grad, gain_ffn_grad])[None, :],
        ],
        axis=0,
    )
    late = row_blocks(after(late, packed))
    up_grad, down_grad = up_parts[0], down_parts[0]
    for up_other, down_other in zip(up_got, down_got):
        up_grad = up_grad + up_other.astype(float_type)
        down_grad = down_grad + down_other.astype(float_type)

    def member_sum(part):
        return summed_shares(part.reshape(members, -1, model_width), "hs")

    out_proj_sum = member_sum(block_mm(gated_blocks, mixer_grad_all))
    gate_sum = member_sum(block_mm(gate_blocks, normed_all))
    packed_sum = row_shares(packed)
    inner_sum = member_sum(block_mm(inner_blocks, normed_all))
    late_sum = row_shares(late)
    given = jnp.where(upper, inner_sum, gate_sum).astype(low_type)
    kept = jnp.where(upper, gate_sum, inner_sum)
    taken = crossed(given, "ep", half).astype(float_type)
    in_proj_sum = jnp.concatenate(
        [jnp.where(upper, taken, kept), jnp.where(upper, kept, taken)], axis=0
    ).T
    cut, at = [], 0
    for piece in pieces:
        cut.append(packed_sum[at : at + piece.shape[0]])
        at += piece.shape[0]
    return (
        block_out,
        tokens_grad,
        late_sum[CONV + 1],
        cut[5].T.reshape(-1),
        in_proj_sum,
        late_sum[:CONV],
        late_sum[CONV],
        cut[0].T,
        cut[1],
        cut[3][0],
        cut[2].T,
        cut[4][0],
        out_proj_sum,
        up_grad[None],
        down_grad[None],
    )


def solution(mesh):
    return jax.shard_map(
        body,
        mesh=mesh,
        in_specs=(
            P(("ep", "hs"), None),
            P(("ep", "hs")),
            P(("ep", "hs")),
            P(("ep", "hs")),
            P(("ep", "hs")),
            P(),
            P(),
            P(),
            P(),
            P(),
            P(),
            P(),
            P(),
            P(),
            P(),
            P(),
            P(),
            P("ep", None, "hs"),
            P("ep", "hs", None),
            P(("ep", "hs"), None),
        ),
        out_specs=(
            P(("ep", "hs"), None),
            P(("ep", "hs"), None),
            P(("ep", "hs")),
            P(("ep", "hs")),
            P(None, ("ep", "hs")),
            P(None, ("ep", "hs")),
            P(("ep", "hs")),
            P(("ep", "hs"), None),
            P(None, ("ep", "hs")),
            P(("ep", "hs")),
            P(("ep", "hs"), None),
            P(("ep", "hs")),
            P(("ep", "hs"), None),
            P("ep", None, "hs"),
            P("ep", "hs", None),
        ),
        check_vma=False,
    )
```

time: 2310 us -> 611 us (0.26)
  waiting for transfers between devices: 919 us -> 150 us
  local copies, waits for them, and re-layouts: 644 us -> 55.9 us
  other arithmetic: 481 us -> 46.1 us
  Pallas kernels: 0 us -> 108 us
  starting transfers between devices: 18.4 us -> 78.8 us
  blocking collectives: 93.5 us -> 34 us
    unnamed x13 -> x4, waiting for transfers between devices: 461 us -> 0.73 us
    reduce_scatter x3 -> x0, waiting for transfers between devices: 373 us -> none  [the longest x1 227 us: body(): lax.psum_scatter(in_proj_grad, ('ep', 'hs'), scatter_dimension=1, tiled=T...]
    squeeze x192 -> x1, local copies, waits for them, and re-layouts: 228 us -> 0.52 us  [body(): late_sum[CONV]]
    reduce_sum x50 -> x4, other arithmetic: 207 us -> 5.01 us  [the longest x1 3.41 us: fold_maps(): summed = jnp.sum(wide, axis=4)]
    dynamic_update_slice x112 -> x0, local copies, waits for them, and re-layouts: 115 us -> none  [the longest x96 62.7 us: block_outputs(): _, readout = lax.scan(jax.checkpoint(advance), opening, sequence)]
    pallas_call x0 -> x4, Pallas kernels: none -> 108 us  [call(): return lambda *operands: run(*operands, *waits)]
    pad x31 -> x0, local copies, waits for them, and re-layouts: 107 us -> none  [block_summaries(): return lax.associative_scan(join_forward, (block_spans, block_ends), axis=0)]
    ppermute x0 -> x22, waiting for transfers between devices: none -> 98.3 us  [the longest x7 74.1 us: crossed(): lax.ppermute(block, axis, [(i, i ^ mask) for i in range(lax.axis_size(axi...]
  transfers between devices with their start and end apart: 14 -> 37, of which waited for: 9 -> 17; matrix products, arithmetic and copies ran while one was open for 4% -> 32% of each run, Pallas kernels for 0% -> 18%
where the time goes in v2:
time: 611 us; the launch traced here: 600 us
  waiting for transfers between devices  150 us (25%)
  matrix products  110 us (18%)
  Pallas kernels  108 us (18%)
  starting transfers between devices  78.8 us (13%)
  local copies, waits for them, and re-layouts  55.9 us (9%)
  other arithmetic  46.1 us (8%)
  blocking collectives  34 us (6%)
  between operations  17.1 us (3%)
    pallas_call x4, Pallas kernels, call(): return lambda *operands: run(*operands, *waits)  108 us
    ppermute x7, waiting for transfers between devices, crossed(): lax.ppermute(block, axis, [(i, i ^ mask) for i in range(lax.axis_size(axi...  74.1 us
    all_to_all x9, waiting for transfers between devices, blocks_home(): return lax.all_to_all(values, 'ep', split_axis=0, concat_axis=0, tiled=True)  51.1 us
    all_to_all x9, starting transfers between devices, blocks_home(): return lax.all_to_all(values, 'ep', split_axis=0, concat_axis=0, tiled=True)  37.7 us
    dot_general x10, matrix products, mm(): return jnp.dot(left, right, preferred_element_type=jnp.float32)  35.1 us
    dot_general x9, matrix products, mm_t(): lax.dot_general(left, right, LAST_DIMS, preferred_element_type=jnp.float32)  33.2 us
    ppermute x15, starting transfers between devices, summed_shares(): lax.ppermute(share.astype(jnp.bfloat16), axis, route).astype(jnp.float32)  25.9 us
    dot_general x8, matrix products, t_mm(): lax.dot_general(left, right, ROWS_FIRST, preferred_element_type=jnp.float32)  25.7 us
  transfers between devices with their start and end apart: 37, of which 17 were waited for; matrix products, arithmetic and copies ran while one was open for 32% of the time, Pallas kernels for 18%

profile of v2, /device:TPU:0, one launch (start us, length us, event | category | flops | bytes accessed | tf_op | source)
XLA Modules:
  0.0 600.2 jit_solution(16669357687242408558)
XLA Ops:
  13.6 6.2 %fusion.170 = f32[256,4608]{1,0:T(8,128)S(1)} fusion(bf16[256,1152]{1,0:T(8,128)(2,1)S(1)} %fusion.63, bf16[1152,4608]{1,0:T(8,128)(2,1)} %param.26), kind=kOutput, calls=%fused_computation.307 | convolution fusion | flops 2717908992 | bytes 15925248 | tf_op jit(solution)/shard_map/dot_general | solution.py:455
  24.3 5.1 collective-permute-start
  33.3 7.3 %fusion.18 = (f32[256,2304]{1,0:T(8,128)S(1)}, f32[256,2304]{1,0:T(8,128)}) fusion(f32[256]{0:T(256)S(1)} %get-tuple-element.222, f32[256,2304]{1,0:T(8,128)} %copy-done.11, f32[3,2304]{1,0:T(4,128)S(1)} %collective-permute-done, f32[2304]{0:T(1024)S(1)} %get-tuple-element.213, f32[256]{0:T(256)S(1)} %get-tuple-element.223, f32[2304]{0:T(1024)S(1)} %get-tuple-element.214, ...), kind=kLoop, calls=%fused_computation.48 | loop fusion | flops 10616832 | bytes 7154688 | tf_op jit(solution)/shard_map/jvp(jit(silu))/mul | solution.py:447
  45.1 4.8 fusion.17
  52.6 14.4 %scan_ends.1 = (f32[128,2304]{1,0:T(8,128)}, f32[8,2304]{1,0:T(8,128)}, f32[16,2304]{1,0:T(8,128)}, f32[1,2304]{1,0:T(1,128)}) custom-call(f32[256,2304]{1,0:T(8,128)} %copy-done.1, f32[256,2304]{1,0:T(8,128)} %get-tuple-element.257.refs_1_.refs_3_, f32[32,16,8,128]{3,2,1,0:T(8,128)} %broadcast_in_dim.20.refs_2_, ...), custom_call_target="tpu_custom_call" | custom-call | bytes 45000000 | tf_op jit(solution)/shard_map/scan_ends/pallas_call | solution.py:279
  68.8 20.0 %all_gather.28 = bf16[4,19,2304]{2,1,0:T(8,128)(2,1)S(1)} all-gather(bf16[1,19,2304]{2,1,0:T(8,128)(2,1)S(1)} %pad_maximum_fusion.3), channel_id=1, replica_groups=mesh['ep'=8,'hs'=4] {'hs'}, dimensions={0}, use_global_device_ids=true | all-gather | bytes 437760 | tf_op jit(solution)/shard_map/all_gather | solution.py:406
  92.6 20.5 %scan_outputs.1 = (f32[256,2304]{1,0:T(8,128)}, bf16[256,2304]{1,0:T(8,128)(2,1)}) custom-call(f32[256,2304]{1,0:T(8,128)} %copy-done.1, f32[256,2304]{1,0:T(8,128)} %get-tuple-element.257.refs_1_.refs_3_, f32[32,16,8,128]{3,2,1,0:T(8,128)} %broadcast_in_dim.20.refs_2_, f32[32,16,8,128]{3,2,1,0:T(8,128)} %broadcast_in_dim.21.refs_3_.refs_4_, ...), custom_call_target="tpu_custom_call" | custom-call | bytes 60000000 | tf_op jit(solution)/shard_map/scan_outputs/pallas_call | solution.py:279
  124.8 10.8 %all-to-all-done = bf16[8,40,1152]{2,1,0:T(8,128)(2,1)} async-done(((bf16[8,40,1152]{2,1,0:T(8,128)(2,1)}), bf16[8,40,1152]{2,1,0:T(8,128)(2,1)}, u32[]{:S(2)}, u32[]{:S(2)}) %all-to-all-start) | async-done | bytes 737312 | tf_op jit(solution)/shard_map/all_to_all | solution.py:507
  141.9 11.7 %all-to-all-done.1 = bf16[8,40,1152]{2,1,0:T(8,128)(2,1)S(1)} async-done(((bf16[8,40,1152]{2,1,0:T(8,128)(2,1)}), bf16[8,40,1152]{2,1,0:T(8,128)(2,1)S(1)}, u32[]{:S(2)}, u32[]{:S(2)}) %all-to-all-start.1) | async-done | bytes 737312 | tf_op jit(solution)/shard_map/all_to_all | solution.py:507
  153.7 13.3 %collective-permute-done.1 = bf16[320,1152]{1,0:T(8,128)(2,1)} collective-permute-done((bf16[320,1152]{1,0:T(8,128)(2,1)}, bf16[320,1152]{1,0:T(8,128)(2,1)}, u32[]{:S(2)}, u32[]{:S(2)}) %collective-permute-start.1) | collective-permute-done | bytes 737312 | tf_op jit(solution)/shard_map/ppermute | solution.py:380
  180.4 21.5 %collective-permute-done.2 = bf16[320,1152]{1,0:T(8,128)(2,1)} collective-permute-done((bf16[320,1152]{1,0:T(8,128)(2,1)S(1)}, bf16[320,1152]{1,0:T(8,128)(2,1)}, u32[]{:S(2)}, u32[]{:S(2)}) %collective-permute-start.2) | collective-permute-done | bytes 737312 | tf_op jit(solution)/shard_map/ppermute | solution.py:380
  221.4 30.3 %collective-permute-done.3 = bf16[320,1152]{1,0:T(8,128)(2,1)S(1)} collective-permute-done((bf16[320,1152]{1,0:T(8,128)(2,1)S(1)}, bf16[320,1152]{1,0:T(8,128)(2,1)S(1)}, u32[]{:S(2)}, u32[]{:S(2)}) %collective-permute-start.3) | collective-permute-done | bytes 737312 | tf_op jit(solution)/shard_map/ppermute | solution.py:380
  252.7 5.0 all-to-all-start.2
  262.3 5.2 collective-permute-done.4
  270.7 5.0 all-to-all-start.3
  282.8 4.8 all-to-all-done.3
  297.3 5.8 fusion.171.refs_0_
  303.2 5.7 all-to-all-done.4.refs_7_
  310.0 15.9 %scan_adjoints.1 = (f32[256,2304]{1,0:T(8,128)}, bf16[256,2304]{1,0:T(8,128)(2,1)}, f32[128,2304]{1,0:T(8,128)}, f32[8,2304]{1,0:T(8,128)}, f32[16,2304]{1,0:T(8,128)}) custom-call(f32[256,2304]{1,0:T(8,128)} %fusion.171.refs_0_, f32[256,2304]{1,0:T(8,128)} %get-tuple-element.224.refs_10_.refs_1_, f32[256,2304]{1,0:T(8,128)} %get-tuple-element.61.refs_2_, ...), custom_call_target="tpu_custom_call" | custom-call | bytes 51000000 | tf_op jit(solution)/shard_map/scan_adjoints/pallas_call | solution.py:279
  326.9 14.0 %all-gather = bf16[64,2304]{1,0:T(8,128)(2,1)S(1)} all-gather(bf16[16,2304]{1,0:T(8,128)(2,1)S(1)} %convert_element_type.277), channel_id=2, replica_groups=mesh['ep'=8,'hs'=4] {'hs'}, dimensions={0}, use_global_device_ids=true | all-gather | bytes 368640 | tf_op jit(solution)/shard_map/all_gather | solution.py:417
  350.4 57.7 %scan_grads.1 = (f32[256,2304]{1,0:T(8,128)}, f32[256,2304]{1,0:T(8,128)}, f32[2,32,16,8,128]{4,3,2,1,0:T(8,128)}, f32[16,2304]{1,0:T(8,128)}, f32[1,2304]{1,0:T(1,128)}) custom-call(f32[256,2304]{1,0:T(8,128)} %copy-done.1, f32[256,2304]{1,0:T(8,128)} %get-tuple-element.257.refs_1_.refs_3_, f32[32,16,8,128]{3,2,1,0:T(8,128)} %broadcast_in_dim.20.refs_2_, ...), custom_call_target="tpu_custom_call" | custom-call | bytes 165000000 | tf_op jit(solution)/shard_map/scan_grads/pallas_call | solution.py:279
  416.5 5.8 fusion
  428.8 5.0 multiply_reduce_fusion.3
  455.4 5.5 fusion.4
  466.6 5.0 all-to-all-done.6
  474.9 6.3 %fusion.64 = (f32[1152]{0:T(1024)S(1)}, f32[256]{0:T(256)}, f32[256,1152]{1,0:T(8,128)}) fusion(bf16[256,1152]{1,0:T(8,128)(2,1)S(1)} %copy-done.15, f32[256]{0:T(256)S(1)} %copy-done.89, f32[1152]{0:T(1024)S(1)} %copy-done.66, f32[256,1152]{1,0:T(8,128)} %fusion, bf16[256,2304]{1,0:T(8,128)(2,1)S(1)} %copy-done.33, bf16[1152,4608]{1,0:T(8,128)(2,1)} %param.26), kind=kOutput, calls=%fused_computation.112 | convolution fusion | flops 1361312384 | bytes 9448448 | tf_op jit(solution)/shard_map/dot_general | solution.py:459
  494.8 11.5 %all-to-all-done.7 = bf16[8,198,288]{1,2,0:T(8,128)(2,1)} async-done(((bf16[8,198,288]{1,2,0:T(8,128)(2,1)}), bf16[8,198,288]{1,2,0:T(8,128)(2,1)}, u32[]{:S(2)}, u32[]{:S(2)}) %all-to-all-start.7) | async-done | bytes 912416 | tf_op jit(solution)/shard_map/all_to_all | solution.py:507
  512.9 6.1 %fusion.5 = f32[1,768,1152]{2,1,0:T(8,128)} fusion(bf16[768,1152]{1,0:T(8,128)(2,1)} %collective-permute-done.23, bf16[320,1152]{1,0:T(8,128)(2,1)} %collective-permute-done.2, bf16[320,1152]{1,0:T(8,128)(2,1)} %bitcast.249, f32[640,768]{1,0:T(8,128)} %fusion.45), kind=kOutput, calls=%fused_computation.12 | convolution fusion | flops 1141604352 | bytes 8749056 | tf_op jit(solution)/shard_map/dot_general | solution.py:463
  547.7 5.7 collective-permute-start.13
  554.0 8.6 %collective-permute-done.17 = bf16[72,1152]{1,0:T(8,128)(2,1)S(1)} collective-permute-done((bf16[72,1152]{1,0:T(8,128)(2,1)S(1)}, bf16[72,1152]{1,0:T(8,128)(2,1)S(1)}, u32[]{:S(2)}, u32[]{:S(2)}) %collective-permute-start.17) | collective-permute-done | bytes 165920 | tf_op jit(solution)/shard_map/ppermute | solution.py:397
  562.7 5.4 collective-permute-done.14
  583.5 8.9 %collective-permute-done.21 = bf16[72,1152]{1,0:T(8,128)(2,1)S(1)} collective-permute-done((bf16[72,1152]{1,0:T(8,128)(2,1)S(1)}, bf16[72,1152]{1,0:T(8,128)(2,1)S(1)}, u32[]{:S(2)}, u32[]{:S(2)}) %collective-permute-start.21) | collective-permute-done | bytes 165920 | tf_op jit(solution)/shard_map/ppermute | solution.py:397
  (425 shorter events, 224.3 us)
Async XLA Ops:
  7.2 83.4 %all-gather.8.cloned.1.call-start = ((), (), s32[]{:S(2)}) async-start(), calls=%async_computation.9 | async-start | bytes 5308416 | tf_op jit(solution)/shard_map/all_gather | solution.py:518
  8.0 163.6 %all-gather.10.cloned.1.call-start = ((), (), s32[]{:S(2)}) async-start(), calls=%async_computation.10 | async-start | bytes 5308416 | tf_op jit(solution)/shard_map/all_gather | solution.py:519
  119.3 16.3 %all-to-all-start = ((bf16[8,40,1152]{2,1,0:T(8,128)(2,1)}), bf16[8,40,1152]{2,1,0:T(8,128)(2,1)}, u32[]{:S(2)}, u32[]{:S(2)}) async-start(bf16[8,40,1152]{2,1,0:T(8,128)(2,1)} %bitcast.14), calls=%async_computation | async-start | bytes 1474560 | tf_op jit(solution)/shard_map/all_to_all | solution.py:507
  135.6 31.3 %collective-permute-start.1 = (bf16[320,1152]{1,0:T(8,128)(2,1)}, bf16[320,1152]{1,0:T(8,128)(2,1)}, u32[]{:S(2)}, u32[]{:S(2)}) collective-permute-start(bf16[320,1152]{1,0:T(8,128)(2,1)} %bitcast.15), channel_id=1, source_target_pairs={{0,2},{1,3},{2,0},{3,1},{4,6},{5,7},{6,4},{7,5},{8,10},{9,11},{10,... | collective-permute-start | bytes 2211848 | tf_op jit(solution)/shard_map/ppermute | solution.py:380
  138.1 15.6 %all-to-all-start.1 = ((bf16[8,40,1152]{2,1,0:T(8,128)(2,1)}), bf16[8,40,1152]{2,1,0:T(8,128)(2,1)S(1)}, u32[]{:S(2)}, u32[]{:S(2)}) async-start(bf16[8,40,1152]{2,1,0:T(8,128)(2,1)} %bitcast.20), calls=%async_computation.1 | async-start | bytes 1474560 | tf_op jit(solution)/shard_map/all_to_all | solution.py:507
  141.6 389.4 %all-gather.12.cloned.1.call-start = ((), (), s32[]{:S(2)}) async-start(), calls=%async_computation.11 | async-start | bytes 5308416 | tf_op jit(solution)/shard_map/all_gather | solution.py:600
  166.9 35.0 %collective-permute-start.2 = (bf16[320,1152]{1,0:T(8,128)(2,1)S(1)}, bf16[320,1152]{1,0:T(8,128)(2,1)}, u32[]{:S(2)}, u32[]{:S(2)}) collective-permute-start(bf16[320,1152]{1,0:T(8,128)(2,1)S(1)} %bitcast.245), channel_id=1, source_target_pairs={{0,2},{1,3},{2,0},{3,1},{4,6},{5,7},{6,4},{7,5},{8,10},{9,11},{10,... | collective-permute-start | bytes 2211848 | tf_op jit(solution)/shard_map/ppermute | solution.py:380
  201.9 49.8 %collective-permute-start.3 = (bf16[320,1152]{1,0:T(8,128)(2,1)S(1)}, bf16[320,1152]{1,0:T(8,128)(2,1)S(1)}, u32[]{:S(2)}, u32[]{:S(2)}) collective-permute-start(bf16[320,1152]{1,0:T(8,128)(2,1)S(1)} %slice.316), channel_id=1, source_target_pairs={{0,2},{1,3},{2,0},{3,1},{4,6},{5,7},{6,4},{7,5},{8,10},{9,11},{10,... | collective-permute-start | bytes 2211848 | tf_op jit(solution)/shard_map/ppermute | solution.py:380
  213.9 53.6 %collective-permute-start.4 = (bf16[320,1152]{1,0:T(8,128)(2,1)}, bf16[320,1152]{1,0:T(8,128)(2,1)}, u32[]{:S(2)}, u32[]{:S(2)}) collective-permute-start(bf16[320,1152]{1,0:T(8,128)(2,1)} %slice.315), channel_id=1, source_target_pairs={{0,2},{1,3},{2,0},{3,1},{4,6},{5,7},{6,4},{7,5},{8,10},{9,11},{10,... | collective-permute-start | bytes 2211848 | tf_op jit(solution)/shard_map/ppermute | solution.py:380
  252.7 17.1 %all-to-all-start.2 = ((bf16[8,40,1152]{2,1,0:T(8,128)(2,1)}), bf16[8,40,1152]{2,1,0:T(8,128)(2,1)S(1)}, u32[]{:S(2)}, u32[]{:S(2)}) async-start(bf16[8,40,1152]{2,1,0:T(8,128)(2,1)} %bitcast.235), calls=%async_computation.2 | async-start | bytes 1474560 | tf_op jit(solution)/shard_map/all_to_all | solution.py:507
  270.7 17.0 %all-to-all-start.3 = ((bf16[8,40,1152]{2,1,0:T(8,128)(2,1)}), bf16[8,40,1152]{2,1,0:T(8,128)(2,1)S(1)}, u32[]{:S(2)}, u32[]{:S(2)}) async-start(bf16[8,40,1152]{2,1,0:T(8,128)(2,1)} %bitcast.234), calls=%async_computation.3 | async-start | bytes 1474560 | tf_op jit(solution)/shard_map/all_to_all | solution.py:507
  288.6 20.3 %all-to-all-start.4 = ((bf16[8,288,256]{2,1,0:T(8,128)(2,1)}), bf16[8,288,256]{2,1,0:T(8,128)(2,1)S(1)}, u32[]{:S(2)}, u32[]{:S(2)}) async-start(bf16[8,288,256]{2,1,0:T(8,128)(2,1)} %bitcast.229), calls=%async_computation.4 | async-start | bytes 2359296 | tf_op jit(solution)/shard_map/all_to_all | solution.py:507
  345.4 76.9 %collective-permute-start.5 = (bf16[1152,768]{1,0:T(8,128)(2,1)}, bf16[1152,768]{1,0:T(8,128)(2,1)}, u32[]{:S(2)}, u32[]{:S(2)}) collective-permute-start(bf16[1152,768]{1,0:T(8,128)(2,1)} %convolution_convert_fusion.2), channel_id=1, source_target_pairs={{0,1},{1,0},{2,3},{3,2},{4,5},{5,4},{6,7},{7,6},{8,9},{9,8},{10,11... | collective-permute-start | bytes 5308424 | tf_op jit(solution)/shard_map/ppermute | solution.py:380
  345.9 76.3 %all-to-all-start.5 = ((bf16[8,288,256]{2,1,0:T(8,128)(2,1)}), bf16[8,288,256]{2,1,0:T(8,128)(2,1)}, u32[]{:S(2)}, u32[]{:S(2)}) async-start(bf16[8,288,256]{2,1,0:T(8,128)(2,1)} %bitcast.31), calls=%async_computation.5 | async-start | bytes 2359296 | tf_op jit(solution)/shard_map/all_to_all | solution.py:507
  350.2 223.5 %all-gather.14.cloned.1.call-start = ((), (), s32[]{:S(2)}) async-start(), calls=%async_computation.12 | async-start | bytes 5308416 | tf_op jit(solution)/shard_map/all_gather | solution.py:650
  436.2 76.7 %collective-permute-start.23 = (bf16[768,1152]{1,0:T(8,128)(2,1)}, bf16[768,1152]{1,0:T(8,128)(2,1)}, u32[]{:S(2)}, u32[]{:S(2)}) collective-permute-start(bf16[768,1152]{1,0:T(8,128)(2,1)} %convolution_convert_fusion.1), channel_id=1, source_target_pairs={{0,1},{1,0},{2,3},{3,2},{4,5},{5,4},{6,7},{7,6},{8,9},{9,8},{10,11... | collective-permute-start | bytes 5308424 | tf_op jit(solution)/shard_map/ppermute | solution.py:380
  450.2 21.3 %all-to-all-start.6 = ((bf16[8,288,256]{2,1,0:T(8,128)(2,1)}), bf16[8,288,256]{2,1,0:T(8,128)(2,1)}, u32[]{:S(2)}, u32[]{:S(2)}) async-start(bf16[8,288,256]{2,1,0:T(8,128)(2,1)} %bitcast.36), calls=%async_computation.6 | async-start | bytes 2359296 | tf_op jit(solution)/shard_map/all_to_all | solution.py:507
  485.2 21.1 %all-to-all-start.7 = ((bf16[8,198,288]{1,2,0:T(8,128)(2,1)}), bf16[8,198,288]{1,2,0:T(8,128)(2,1)}, u32[]{:S(2)}, u32[]{:S(2)}) async-start(bf16[8,198,288]{1,2,0:T(8,128)(2,1)} %copy.118), calls=%async_computation.7 | async-start | bytes 2359296 | tf_op jit(solution)/shard_map/all_to_all | solution.py:507
  507.8 15.3 %collective-permute-start.12 = (bf16[198,72]{0,1:T(8,128)(2,1)S(1)}, bf16[198,72]{0,1:T(8,128)(2,1)S(1)}, u32[]{:S(2)}, u32[]{:S(2)}) collective-permute-start(bf16[198,72]{0,1:T(8,128)(2,1)S(1)} %get-tuple-element.243), channel_id=1, source_target_pairs={{0,3},{1,0},{2,1},{3,2},{4,7},{5,4},{6,5},{7,6},{8,11},{9,8},{10,9... | collective-permute-start | bytes 85544 | tf_op jit(solution)/shard_map/ppermute | solution.py:397
  510.3 12.8 %collective-permute-start.11 = (bf16[198,72]{0,1:T(8,128)(2,1)S(1)}, bf16[198,72]{0,1:T(8,128)(2,1)S(1)}, u32[]{:S(2)}, u32[]{:S(2)}) collective-permute-start(bf16[198,72]{0,1:T(8,128)(2,1)S(1)} %get-tuple-element.244), channel_id=1, source_target_pairs={{0,2},{1,3},{2,0},{3,1},{4,6},{5,7},{6,4},{7,5},{8,10},{9,11},{10,... | collective-permute-start | bytes 85544 | tf_op jit(solution)/shard_map/ppermute | solution.py:397
  511.0 12.2 %collective-permute-start.10 = (bf16[198,72]{0,1:T(8,128)(2,1)S(1)}, bf16[198,72]{0,1:T(8,128)(2,1)S(1)}, u32[]{:S(2)}, u32[]{:S(2)}) collective-permute-start(bf16[198,72]{0,1:T(8,128)(2,1)S(1)} %get-tuple-element.242), channel_id=1, source_target_pairs={{0,1},{1,2},{2,3},{3,0},{4,5},{5,6},{6,7},{7,4},{8,9},{9,10},{10,1... | collective-permute-start | bytes 85544 | tf_op jit(solution)/shard_map/ppermute | solution.py:397
  528.4 14.9 %collective-permute-start.9 = (bf16[6,72]{1,0:T(8,128)(2,1)S(1)}, bf16[6,72]{1,0:T(8,128)(2,1)S(1)}, u32[]{:S(2)}, u32[]{:S(2)}) collective-permute-start(bf16[6,72]{1,0:T(8,128)(2,1)S(1)} %bitcast.260), channel_id=1, source_target_pairs={{0,3},{1,0},{2,1},{3,2},{4,7},{5,4},{6,5},{7,6},{8,11},{9,8},{10,9... | collective-permute-start | bytes 2600 | tf_op jit(solution)/shard_map/ppermute | solution.py:397
  530.3 13.2 %collective-permute-start.8 = (bf16[6,72]{1,0:T(8,128)(2,1)S(1)}, bf16[6,72]{1,0:T(8,128)(2,1)S(1)}, u32[]{:S(2)}, u32[]{:S(2)}) collective-permute-start(bf16[6,72]{1,0:T(8,128)(2,1)S(1)} %bitcast.259), channel_id=1, source_target_pairs={{0,2},{1,3},{2,0},{3,1},{4,6},{5,7},{6,4},{7,5},{8,10},{9,11},{10,... | collective-permute-start | bytes 2600 | tf_op jit(solution)/shard_map/ppermute | solution.py:397
  530.8 16.4 %collective-permute-start.7 = (bf16[6,72]{1,0:T(8,128)(2,1)S(1)}, bf16[6,72]{1,0:T(8,128)(2,1)S(1)}, u32[]{:S(2)}, u32[]{:S(2)}) collective-permute-start(bf16[6,72]{1,0:T(8,128)(2,1)S(1)} %bitcast.258), channel_id=1, source_target_pairs={{0,1},{1,2},{2,3},{3,0},{4,5},{5,6},{6,7},{7,4},{8,9},{9,10},{10,1... | collective-permute-start | bytes 2600 | tf_op jit(solution)/shard_map/ppermute | solution.py:397
  535.6 12.0 %collective-permute-start.18 = (bf16[72,1152]{1,0:T(8,128)(2,1)S(1)}, bf16[72,1152]{1,0:T(8,128)(2,1)S(1)}, u32[]{:S(2)}, u32[]{:S(2)}) collective-permute-start(bf16[72,1152]{1,0:T(8,128)(2,1)S(1)} %get-tuple-element.236), channel_id=1, source_target_pairs={{0,3},{1,0},{2,1},{3,2},{4,7},{5,4},{6,5},{7,6},{8,11},{9,8},{10,9... | collective-permute-start | bytes 497672 | tf_op jit(solution)/shard_map/ppermute | solution.py:397
  539.6 23.1 %collective-permute-start.17 = (bf16[72,1152]{1,0:T(8,128)(2,1)S(1)}, bf16[72,1152]{1,0:T(8,128)(2,1)S(1)}, u32[]{:S(2)}, u32[]{:S(2)}) collective-permute-start(bf16[72,1152]{1,0:T(8,128)(2,1)S(1)} %get-tuple-element.237), channel_id=1, source_target_pairs={{0,2},{1,3},{2,0},{3,1},{4,6},{5,7},{6,4},{7,5},{8,10},{9,11},{10,... | collective-permute-start | bytes 497672 | tf_op jit(solution)/shard_map/ppermute | solution.py:397
  543.3 19.3 %collective-permute-start.16 = (bf16[72,1152]{1,0:T(8,128)(2,1)S(1)}, bf16[72,1152]{1,0:T(8,128)(2,1)S(1)}, u32[]{:S(2)}, u32[]{:S(2)}) collective-permute-start(bf16[72,1152]{1,0:T(8,128)(2,1)S(1)} %get-tuple-element.235), channel_id=1, source_target_pairs={{0,1},{1,2},{2,3},{3,0},{4,5},{5,6},{6,7},{7,4},{8,9},{9,10},{10,1... | collective-permute-start | bytes 497672 | tf_op jit(solution)/shard_map/ppermute | solution.py:397
  543.5 19.1 %collective-permute-start.15 = (bf16[72,1152]{1,0:T(8,128)(2,1)S(1)}, bf16[72,1152]{1,0:T(8,128)(2,1)S(1)}, u32[]{:S(2)}, u32[]{:S(2)}) collective-permute-start(bf16[72,1152]{1,0:T(8,128)(2,1)S(1)} %get-tuple-element.233), channel_id=1, source_target_pairs={{0,3},{1,0},{2,1},{3,2},{4,7},{5,4},{6,5},{7,6},{8,11},{9,8},{10,9... | collective-permute-start | bytes 497672 | tf_op jit(solution)/shard_map/ppermute | solution.py:397
  547.2 20.8 %collective-permute-start.14 = (bf16[72,1152]{1,0:T(8,128)(2,1)S(1)}, bf16[72,1152]{1,0:T(8,128)(2,1)S(1)}, u32[]{:S(2)}, u32[]{:S(2)}) collective-permute-start(bf16[72,1152]{1,0:T(8,128)(2,1)S(1)} %get-tuple-element.234), channel_id=1, source_target_pairs={{0,2},{1,3},{2,0},{3,1},{4,6},{5,7},{6,4},{7,5},{8,10},{9,11},{10,... | collective-permute-start | bytes 497672 | tf_op jit(solution)/shard_map/ppermute | solution.py:397
  547.7 20.4 %collective-permute-start.13 = (bf16[72,1152]{1,0:T(8,128)(2,1)S(1)}, bf16[72,1152]{1,0:T(8,128)(2,1)S(1)}, u32[]{:S(2)}, u32[]{:S(2)}) collective-permute-start(bf16[72,1152]{1,0:T(8,128)(2,1)S(1)} %get-tuple-element.232), channel_id=1, source_target_pairs={{0,1},{1,2},{2,3},{3,0},{4,5},{5,6},{6,7},{7,4},{8,9},{9,10},{10,1... | collective-permute-start | bytes 497672 | tf_op jit(solution)/shard_map/ppermute | solution.py:397
  577.9 14.5 %collective-permute-start.21 = (bf16[72,1152]{1,0:T(8,128)(2,1)S(1)}, bf16[72,1152]{1,0:T(8,128)(2,1)S(1)}, u32[]{:S(2)}, u32[]{:S(2)}) collective-permute-start(bf16[72,1152]{1,0:T(8,128)(2,1)S(1)} %get-tuple-element.231), channel_id=1, source_target_pairs={{0,2},{1,3},{2,0},{3,1},{4,6},{5,7},{6,4},{7,5},{8,10},{9,11},{10,... | collective-permute-start | bytes 497672 | tf_op jit(solution)/shard_map/ppermute | solution.py:397
  579.4 13.0 %collective-permute-start.20 = (bf16[72,1152]{1,0:T(8,128)(2,1)S(1)}, bf16[72,1152]{1,0:T(8,128)(2,1)S(1)}, u32[]{:S(2)}, u32[]{:S(2)}) collective-permute-start(bf16[72,1152]{1,0:T(8,128)(2,1)S(1)} %get-tuple-element.229), channel_id=1, source_target_pairs={{0,1},{1,2},{2,3},{3,0},{4,5},{5,6},{6,7},{7,4},{8,9},{9,10},{10,1... | collective-permute-start | bytes 497672 | tf_op jit(solution)/shard_map/ppermute | solution.py:397
  (114 other events, 1609.8 us)
Sparse Core Ops, SparseCore 0:
  9.6 52.0 all-gather.7
  63.3 55.2 all-gather.9
  153.8 36.5 all-gather.11
  416.6 39.5 all-gather.13
